TPU v7x, 32 devices: a whole 2x2x4 slice. The times are simulated.
32 devices in a mesh: dp: 16 (over z, x, core), ctx: 2 (over y).
Axes of the slice: x: 2, y: 2, z: 4, core: 2. Of those that a mesh axis runs over, the one named last changes fastest.
Arguments:
- query_vecs: bfloat16 [16, 256, 1024], P('dp', 'ctx'), may hold values from -12 to 12, as said below
- key_vecs: bfloat16 [16, 256, 1024], P('dp', 'ctx'), may hold values from -12 to 12
- value_vecs: bfloat16 [16, 256, 1024], P('dp', 'ctx'), may hold values from -6 to 6
- residual: bfloat16 [16, 256, 2048], P('dp', 'ctx'), may hold values from -45 to 45
- w_out: bfloat16 [1024, 2048], P('dp'), may hold values from -0.75 to 0.75
- norm_gain: float32 [2048], replicated, may hold values from 0.25 to 1.75
- w_gate_up: bfloat16 [16, 2, 2048, 1408], P('dp', None, None, 'ctx'), may hold values from -0.125 to 0.125
- w_down: bfloat16 [16, 1408, 2048], P('dp', 'ctx'), may hold values from -0.15625 to 0.15625
- expert_ids: int32 [16, 256, 6], P('dp', 'ctx'), may hold values from 0 to 15, as said below
- route_gates: float32 [16, 256, 6], P('dp', 'ctx'), may hold values from 0.1 to 0.9
- capacity: int32 [16, 2, 2], P('dp', 'ctx'), may hold values from 12 to 24, as said below
- expert_owner: int32 [16], replicated, may hold values from 0 to 15, each once
Outputs:
- attn_proj: bfloat16 [16, 256, 2048], P('dp', 'ctx')
- expert_sum: bfloat16 [16, 256, 2048], P('dp', 'ctx')
Inputs may be any that keep to these rules, and one draw needn't show every extreme that they name: `query_vecs`: q and k are drawn together. `expert_ids`: each position names 6 different experts; in each aligned block of 128 positions, experts 0 to 1 are each named by at least 24 positions. In each block some expert has capacity 24. `expert_owner`: each index of dp holds one expert.
All inputs are finite; a program needn't handle non-finite values.
Results may differ from a plain program's by a relative error of at most 0.019.
Values may be sent and summed in bfloat16 or wider, within the bound.
No kernel may reach another device: no remote copies, remote signals or barrier semaphores. Data moves between devices by JAX's collectives and lax.ppermute only.
A program may use at most 128 MiB of HBM per device.

v0:
```python
import functools

import jax
import jax.numpy as jnp
from jax import lax
from jax.experimental import pallas as pl
from jax.experimental.pallas import tpu as pltpu
from jax.sharding import PartitionSpec as P

HEADS = 8
HD = 128
PASS_SPECIALISTS = 2
CAP = 24


EPSILON = 1e-06
LOWEST = -1e30


def broadcast(array, axis, root):
    mine = lax.axis_index(axis) == root
    return lax.psum(jnp.where(mine, array, jnp.zeros_like(array)), axis)


def hop(array, axis, size, bit):
    return lax.ppermute(array, axis, [(i, i ^ bit) for i in range(size)])


def route_slots(expert_ids, route_gates, capacity, expert):
    matches = expert_ids == expert
    routed = jnp.any(matches, axis=1)
    gate_value = jnp.sum(jnp.where(matches, route_gates, 0.0), axis=1)
    slot_rank = jnp.cumsum(routed.astype(jnp.int32)) - 1
    kept_mask = routed & (slot_rank < capacity[expert])
    return (slot_rank, kept_mask, gate_value)


def attend(queries, key_block, value_block, visible):
    width = key_block.shape[0]
    token_count = queries.shape[0]
    query_heads = queries.reshape(token_count, HEADS, HD)
    key_heads = key_block.reshape(width, HEADS, HD)
    value_heads = value_block.reshape(width, HEADS, HD)
    gating_logits = jnp.einsum(
        "qhd,khd->qhk", query_heads, key_heads, preferred_element_type=jnp.float32
    ) * HD ** (-0.5)
    gating_logits = jnp.where(visible[:, None, :], gating_logits, -jnp.inf)
    row_top = jnp.max(gating_logits, axis=-1)
    weights = jnp.exp(gating_logits - row_top[:, :, None])
    denominator = jnp.sum(weights, axis=-1)
    weighted = jnp.einsum(
        "qhk,khd->qhd",
        weights.astype(jnp.bfloat16),
        value_heads,
        preferred_element_type=jnp.float32,
    )
    attended = (weighted / denominator[:, :, None]).astype(jnp.bfloat16)
    return attended.reshape(token_count, HEADS * HD)


def feed_forward(rows, gate_up, down_part):
    gate_proj = jnp.dot(rows, gate_up[0], preferred_element_type=jnp.float32)
    up_proj = jnp.dot(rows, gate_up[1], preferred_element_type=jnp.float32)
    hidden = (jax.nn.silu(gate_proj) * up_proj).astype(jnp.bfloat16)
    return jnp.dot(hidden, down_part, preferred_element_type=jnp.float32).astype(jnp.bfloat16)


def normalise(attn_proj, residual, norm_gain):
    combined = residual.astype(jnp.float32) + attn_proj.astype(jnp.float32)
    return (
        combined
        * lax.rsqrt(jnp.mean(combined * combined, axis=-1, keepdims=True) + EPSILON)
        * norm_gain
    ).astype(jnp.bfloat16)


def pick_rows(routing, normed):
    slot_ids = jnp.arange(CAP)
    select = [
        (slot_rank[None, :] == slot_ids[:, None]) & kept_mask[None, :]
        for slot_rank, kept_mask, _ in routing
    ]
    select = jnp.concatenate(select, axis=0).astype(jnp.bfloat16)
    chosen = jnp.dot(select, normed, preferred_element_type=jnp.float32).astype(jnp.bfloat16)
    return chosen.reshape(PASS_SPECIALISTS, CAP, normed.shape[1])


def combine_rows(routing, produced):
    slot_ids = jnp.arange(CAP)
    summed = 0.0
    for expert in range(PASS_SPECIALISTS):
        slot_rank, kept_mask, gate_value = routing[expert]
        place = ((slot_rank[:, None] == slot_ids[None, :]) & kept_mask[:, None]).astype(
            jnp.bfloat16
        )
        picked = jnp.dot(place, produced[expert], preferred_element_type=jnp.float32)
        summed = summed + gate_value[:, None] * picked
    return summed.astype(jnp.bfloat16)


def body_move_weights(
    query_vecs,
    key_vecs,
    value_vecs,
    residual,
    w_out,
    norm_gain,
    w_gate_up,
    w_down,
    expert_ids,
    route_gates,
    capacity,
    expert_owner,
):
    token_count = query_vecs.shape[1]
    weights_in = []
    for expert in range(PASS_SPECIALISTS):
        weights_in.append(
            (
                broadcast(w_gate_up[0], "dp", expert_owner[expert]),
                broadcast(w_down[0], "dp", expert_owner[expert]),
            )
        )
    keys = lax.all_gather(key_vecs[0], "ctx", axis=0, tiled=True)
    values = lax.all_gather(value_vecs[0], "ctx", axis=0, tiled=True)
    first_row = lax.axis_index("ctx") * token_count
    query_pos = first_row + jnp.arange(token_count)
    visible = jnp.arange(keys.shape[0])[None, :] <= query_pos[:, None]
    attended = attend(query_vecs[0], keys, values, visible)
    projected = jnp.dot(
        attended,
        lax.all_gather(w_out, "dp", axis=0, tiled=True),
        preferred_element_type=jnp.float32,
    )
    attn_proj = projected.astype(jnp.bfloat16)
    normed = normalise(attn_proj, residual[0], norm_gain)
    routing = [
        route_slots(expert_ids[0], route_gates[0], capacity[0, 0], expert)
        for expert in range(PASS_SPECIALISTS)
    ]
    chosen = pick_rows(routing, normed)
    routed_rows = lax.all_gather(jnp.swapaxes(chosen, 0, 1), "ctx", axis=0, tiled=True)
    outputs = [
        feed_forward(routed_rows[:, expert], *weights_in[expert])
        for expert in range(PASS_SPECIALISTS)
    ]
    expert_out = lax.psum_scatter(
        jnp.stack(outputs, axis=1), "ctx", scatter_dimension=0, tiled=True
    )
    expert_sum = combine_rows(routing, [expert_out[:, e] for e in range(PASS_SPECIALISTS)])
    return (attn_proj[None], expert_sum[None])


CTX, CHIP, CORE, FIRST, FIRST_CAP, SECOND, SECOND_CAP, SAME = range(8)
FIRST_HERE, SECOND_HERE, PASSES, BRANCH, PASS_INFO = range(8, 13)
USE_FAR, NEAR_LAST, NEAR_SECOND, OTHER_NEAR, PASS_COUNT = range(5)


def work_out_places(bits, numbers, info):
    owners = [numbers[k] for k in range(PASS_SPECIALISTS)]
    caps = [numbers[PASS_SPECIALISTS + k] for k in range(PASS_SPECIALISTS)]
    me = lax.axis_index("dp")
    differ = owners[0] ^ owners[1]
    branch = 0
    split_bit = 0
    rest = [bits[1], bits[2]]
    for k in reversed(range(len(bits))):
        parted = (differ & bits[k]) != 0
        branch = jnp.where(parted, k, branch)
        split_bit = jnp.where(parted, bits[k], split_bit)
        others = [bit for bit in bits if bit != bits[k]]
        rest = [jnp.where(parted, others[i], rest[i]) for i in range(2)]
    same = split_bit == 0
    swapped = ((me ^ owners[0]) & split_bit) != 0
    first_offset = me ^ jnp.where(swapped, owners[1], owners[0])
    second_offset = me ^ jnp.where(swapped, owners[0], owners[1])

    def put(place, value):
        info[place] = value.astype(jnp.int32)

    put(CTX, lax.axis_index("ctx"))
    put(CHIP, me >> 1)
    put(CORE, me & 1)
    put(FIRST, jnp.where(swapped, 1, 0))
    put(FIRST_CAP, jnp.where(swapped, caps[1], caps[0]))
    put(SECOND, jnp.where(swapped, 0, 1))
    put(SECOND_CAP, jnp.where(swapped, caps[0], caps[1]))
    put(SAME, jnp.where(same, 1, 0))
    put(FIRST_HERE, jnp.where((first_offset & bits[0]) == 0, 1, 0))
    put(SECOND_HERE, jnp.where((second_offset & bits[0]) == 0, 1, 0))
    put(PASSES, jnp.where(same, 2, 1))
    put(BRANCH, branch)
    pairs = (
        (first_offset, jnp.where(same, first_offset, second_offset)),
        (second_offset, second_offset),
    )
    for k, (offset, other_offset) in enumerate(pairs):
        base = PASS_INFO + k * PASS_COUNT
        put(base + USE_FAR, offset & 1)
        put(base + NEAR_LAST, jnp.where((offset & rest[1]) == 0, 1, 0))
        put(base + NEAR_SECOND, jnp.where((offset & rest[0]) == 0, 1, 0))
        put(base + OTHER_NEAR, jnp.where((other_offset & rest[0]) == 0, 1, 0))


def attend_kernel(bits, numbers, own_vecs, key_before, value_before, ids, gates, *outs):
    attended, select, gate_values, info = outs
    query, key, value = (own_vecs.at[k] for k in range(3))
    work_out_places(bits, numbers, info)
    token_count = query.shape[0]
    row = lax.broadcasted_iota(jnp.int32, (token_count, token_count), 0)
    col = lax.broadcasted_iota(jnp.int32, (token_count, token_count), 1)
    own_visible = col <= row
    before_visible = jnp.broadcast_to(info[CTX], (token_count, token_count)) == 1
    contract_last = (((1,), (1,)), ((), ()))
    for head in range(HEADS):
        span = slice(head * HD, (head + 1) * HD)
        heads = query[:, span]
        own = lax.dot_general(
            heads, key[:, span], contract_last, preferred_element_type=jnp.float32
        )
        before = lax.dot_general(
            heads, key_before[:, span], contract_last, preferred_element_type=jnp.float32
        )
        own = jnp.where(own_visible, own * HD ** (-0.5), -jnp.inf)
        before = jnp.where(before_visible, before * HD ** (-0.5), -jnp.inf)
        top = jnp.maximum(
            jnp.max(own, axis=1, keepdims=True), jnp.max(before, axis=1, keepdims=True)
        )
        own = jnp.exp(own - top)
        before = jnp.exp(before - top)
        total = jnp.sum(own, axis=1, keepdims=True) + jnp.sum(before, axis=1, keepdims=True)
        mixed = jnp.dot(
            own.astype(jnp.bfloat16), value[:, span], preferred_element_type=jnp.float32
        ) + jnp.dot(
            before.astype(jnp.bfloat16), value_before[:, span], preferred_element_type=jnp.float32
        )
        mixed = mixed / total
        swapped = pltpu.roll(mixed, HD // 2, 1)
        mixed = jnp.where(jnp.broadcast_to(info[CORE], mixed.shape) == 0, mixed, swapped)
        attended[head ^ info[CHIP]] = mixed.astype(jnp.bfloat16)

    slot = lax.broadcasted_iota(jnp.int32, (CAP, token_count), 0)
    earlier = (row < col).astype(jnp.bfloat16)
    for k in range(PASS_SPECIALISTS):
        matches = ids[...] == info[FIRST + 2 * k]
        named = jnp.max(matches.astype(jnp.float32), axis=0, keepdims=True)
        gate_row = jnp.sum(jnp.where(matches, gates[...], 0.0), axis=0, keepdims=True)
        gate_values[:, k : k + 1] = jnp.sum(
            jnp.where(row == col, jnp.broadcast_to(gate_row, row.shape), 0.0),
            axis=1,
            keepdims=True,
        )
        routed = jnp.broadcast_to(named, (CAP, token_count))
        rank = jnp.dot(
            routed.astype(jnp.bfloat16), earlier, preferred_element_type=jnp.float32
        ).astype(jnp.int32)
        kept = (routed > 0.0) & (rank == slot) & (rank < info[FIRST_CAP + 2 * k])
        select[k] = kept.astype(jnp.bfloat16)


def add_products(attended, chips, near, far, span, total):
    for pair in range(0, len(chips), 2):
        one, two = chips[pair], chips[pair + 1]
        left = jnp.concatenate([attended[one], attended[two]], axis=1)
        right = jnp.concatenate(
            [near[pair][:, span], far[pair][:, span]]
            + [near[pair + 1][:, span], far[pair + 1][:, span]],
            axis=0,
        )
        product = jnp.dot(left, right, preferred_element_type=jnp.float32)
        total = product if total is None else total + product
    return total


def early_kernel(chips, attended, *refs):
    near, far = refs[: len(chips)], refs[len(chips) : -1]
    total = refs[-1]
    for start in range(0, total.shape[1], 512):
        span = slice(start, start + 512)
        total[:, span] = add_products(attended, chips, near, far, span, None)


def project_kernel(chips, info, attended, residual, gain, select, early, *refs):
    near, far = refs[: len(chips)], refs[len(chips) : 2 * len(chips)]
    attn_proj, kept, sent, second, _, _, combined = refs[-7:]
    token_count, width = residual.shape
    tile = 512
    squares = jnp.zeros((token_count, 1), jnp.float32)
    for start in range(0, width, tile):
        span = slice(start, start + tile)
        total = add_products(attended, chips, near, far, span, early[:, span])
        rounded = total.astype(jnp.bfloat16)
        attn_proj[:, span] = rounded
        added = residual[:, span].astype(jnp.float32) + rounded.astype(jnp.float32)
        combined[:, span] = added
        squares = squares + jnp.sum(added * added, axis=1, keepdims=True)
    scale = lax.rsqrt(squares / width + EPSILON)
    for start in range(0, width, tile):
        span = slice(start, start + tile)
        normed = (combined[:, span] * scale * gain[:, span]).astype(jnp.bfloat16)
        rows = [
            jnp.dot(select[k], normed, preferred_element_type=jnp.float32)
            for k in range(PASS_SPECIALISTS)
        ]
        kept[:, span] = rows[0].astype(jnp.bfloat16)
        second[:, span] = rows[1].astype(jnp.bfloat16)
        use_first = jnp.broadcast_to(info[SAME], rows[0].shape) != 0
        sent[:, span] = jnp.where(use_first, rows[0], rows[1]).astype(jnp.bfloat16)


def combine_kernel(info, step, own, other, last, second, select, gate_values, *outs):
    out, next_last, next_kept, next_sent = outs
    same = info[SAME] != 0
    contract_first = (((0,), (0,)), ((), ()))

    def add_up(first_rows, second_rows):
        total = 0.0
        for k, rows in enumerate((first_rows, second_rows)):
            picked = lax.dot_general(
                select[k], rows, contract_first, preferred_element_type=jnp.float32
            )
            total = total + gate_values[:, k : k + 1] * picked
        return total.astype(jnp.bfloat16)

    @pl.when(jnp.logical_not(same))
    def _():
        for start in range(0, own.shape[1], 512):
            span = slice(start, start + 512)
            out[:, span] = add_up(own[:, span], other[:, span])

    @pl.when(same)
    def _():
        here = jnp.where(step[0] == 0, info[FIRST_HERE], info[SECOND_HERE])
        for start in range(0, own.shape[1], 512):
            span = slice(start, start + 512)
            use_own = jnp.broadcast_to(here, (own.shape[0], 512)) != 0
            served = jnp.where(
                use_own, own[:, span].astype(jnp.float32), other[:, span].astype(jnp.float32)
            ).astype(jnp.bfloat16)
            out[:, span] = add_up(last[:, span], served)
            next_last[:, span] = served
            next_kept[:, span] = second[:, span]
            next_sent[:, span] = second[:, span]


def expert_kernel(
    info,
    step,
    rows,
    gate_up_near,
    gate_up_far,
    down_near,
    down_far,
    made,
    masks,
    gate_up,
    down,
    sums,
    hidden,
    sems,
):
    units, width = down.shape
    piece = 512
    starts = list(range(0, width, piece))

    def copies(gate_up_from, down_from):
        spans = [pl.ds(start, piece) for start in starts]
        out = [
            pltpu.make_async_copy(gate_up_from.at[:, :, span], gate_up.at[:, :, span], sems.at[k])
            for k, span in enumerate(spans)
        ]
        return out + [pltpu.make_async_copy(down_from, down, sems.at[len(starts)])]

    base = PASS_INFO + PASS_COUNT * step[0]
    use_far = info[base + USE_FAR]

    def start_copy(stage):
        @pl.when(use_far == 0)
        def _():
            copies(gate_up_near, down_near)[stage].start()

        @pl.when(use_far != 0)
        def _():
            copies(gate_up_far, down_far)[stage].start()

    start_copy(0)
    start_copy(1)
    for k in (NEAR_LAST, NEAR_SECOND, OTHER_NEAR):
        masks[k] = jnp.broadcast_to(info[base + k].astype(jnp.float32), masks.shape[1:])

    arrived = copies(gate_up_near, down_near)
    contract_last = (((1,), (1,)), ((), ()))
    for k, start in enumerate(starts):
        span = slice(start, start + piece)
        arrived[k].wait()
        if k + 2 < len(arrived):
            start_copy(k + 2)
        product = lax.dot_general(
            gate_up[:, :, span].reshape(2 * units, piece),
            rows[:, span],
            contract_last,
            preferred_element_type=jnp.float32,
        )
        if k == 0:
            sums[...] = product
        else:
            sums[...] += product
    for start in range(0, units, 256):
        stop = min(start + 256, units)
        gate_proj, up_proj = sums[start:stop], sums[units + start : units + stop]
        made_hidden = gate_proj / (1.0 + jnp.exp(-gate_proj)) * up_proj
        hidden[:, start:stop] = jnp.transpose(made_hidden).astype(jnp.bfloat16)
    arrived[-1].wait()
    for start in range(0, width, 512):
        span = slice(start, start + 512)
        made[:, span] = jnp.dot(
            hidden[...], down[:, span], preferred_element_type=jnp.float32
        ).astype(jnp.bfloat16)


def gather_rows(kept, sent, first, bits, dp_size):
    second, last = bits

    beside = hop(kept, "dp", dp_size, second)
    across = hop(sent, "dp", dp_size, first)
    beyond = hop(sent, "dp", dp_size, first | second)
    unit = jnp.concatenate([kept, beside, across, beyond], axis=0)
    half = unit.shape[1] // 2
    left, right = unit[:, :half], unit[:, half:]
    left = jnp.stack([left, hop(left, "dp", dp_size, last)])
    right = jnp.stack([right, hop(right, "ctx", 2, 1)])
    left = jnp.stack([left, hop(left, "ctx", 2, 1)])
    right = jnp.stack([right, hop(right, "dp", dp_size, last)], axis=1)
    rows = jnp.concatenate([left, right], axis=-1)
    return rows.reshape(-1, rows.shape[-1])


def scatter_rows(rows, first, bits, dp_size, masks):
    second, last = bits
    half = rows.shape[1] // 2
    rows = rows.reshape(2, 2, -1, rows.shape[1])
    left, right = rows[..., :half], rows[..., half:]

    def add(kept, came):
        return (kept.astype(jnp.float32) + came.astype(jnp.float32)).astype(jnp.bfloat16)

    left = add(left[0], hop(left[1], "ctx", 2, 1))
    right = jnp.where(masks[NEAR_LAST, :, half:] != 0, right[:, 0], hop(right[:, 1], "dp", dp_size, last))
    left = jnp.where(masks[NEAR_LAST, :, :half] != 0, left[0], hop(left[1], "dp", dp_size, last))
    right = add(right[0], hop(right[1], "ctx", 2, 1))
    unit = jnp.concatenate([left, right], axis=-1)
    here, beside, across, beyond = lax.optimization_barrier(jnp.split(unit, 4, axis=0))

    across = hop(across, "dp", dp_size, first)
    beside = hop(beside, "dp", dp_size, second)
    beyond = hop(beyond, "dp", dp_size, first | second)
    return (
        jnp.where(masks[NEAR_SECOND] != 0, here, beside),
        jnp.where(masks[OTHER_NEAR] != 0, across, beyond),
    )


def smem(count):
    return [pl.BlockSpec(memory_space=pltpu.SMEM)] * count


def vmem(count):
    return [pl.BlockSpec(memory_space=pltpu.VMEM)] * count


def body_move_rows(
    query_vecs,
    key_vecs,
    value_vecs,
    residual,
    w_out,
    norm_gain,
    w_gate_up,
    w_down,
    expert_ids,
    route_gates,
    capacity,
    expert_owner,
):
    token_count = query_vecs.shape[1]
    width = residual.shape[2]
    dp_size = lax.axis_size("dp")
    bits = [1 << k for k in reversed(range(1, dp_size.bit_length() - 1))]

    z_far, z_near, x_bit = bits
    z_both = z_far | z_near
    near = {0: w_out}
    for bit in (z_far, z_near, x_bit):
        near[bit] = hop(w_out, "dp", dp_size, bit)
    key_before = lax.ppermute(key_vecs[0], "ctx", [(0, 1)])
    value_before = lax.ppermute(value_vecs[0], "ctx", [(0, 1)])
    own = jnp.stack([query_vecs[0], key_vecs[0], value_vecs[0]])
    numbers = jnp.concatenate([expert_owner[:PASS_SPECIALISTS], capacity[0, 0]])
    (
        near[z_far],
        near[z_near],
        near[x_bit],
        near[0],
        key_before,
        own,
        numbers,
        ids,
        gates,
    ) = lax.optimization_barrier(
        (
            near[z_far],
            near[z_near],
            near[x_bit],
            near[0],
            key_before,
            own,
            numbers,
            jnp.transpose(expert_ids[0]),
            jnp.transpose(route_gates[0]),
        )
    )
    near[z_near | x_bit] = hop(near[z_near], "dp", dp_size, x_bit)
    near[z_both] = hop(near[z_far], "dp", dp_size, z_near)
    near[z_far | x_bit] = hop(near[z_far], "dp", dp_size, x_bit)
    value_before, near[z_both] = lax.optimization_barrier((value_before, near[z_both]))
    attended, select, gate_values, info = pl.pallas_call(
        functools.partial(attend_kernel, bits),
        out_shape=(
            jax.ShapeDtypeStruct((HEADS, token_count, HD), jnp.bfloat16),
            jax.ShapeDtypeStruct((PASS_SPECIALISTS, CAP, token_count), jnp.bfloat16),
            jax.ShapeDtypeStruct((token_count, PASS_SPECIALISTS), jnp.float32),
            jax.ShapeDtypeStruct((PASS_INFO + 2 * PASS_COUNT,), jnp.int32),
        ),
        in_specs=smem(1) + vmem(5),
        out_specs=tuple(vmem(3) + smem(1)),
        cost_estimate=pl.CostEstimate(
            flops=64 * HEADS * HD * 2 * token_count * token_count,
            bytes_accessed=6 * 2 * token_count * HEADS * HD,
            transcendentals=2 * HEADS * token_count * token_count,
        ),
        compiler_params=pltpu.CompilerParams(vmem_limit_bytes=8 * 2**20),
    )(numbers, own, key_before, value_before, ids, gates)
    near[z_both | x_bit] = hop(near[z_both], "dp", dp_size, x_bit)
    (
        near[z_near | x_bit],
        near[z_far | x_bit],
        between,
        attended,
    ) = lax.optimization_barrier(
        (near[z_near | x_bit], near[z_far | x_bit], near[z_both], attended)
    )
    far = {}
    for bit in (0, z_far, z_near, x_bit, z_near | x_bit, z_far | x_bit, z_both | x_bit):
        far[bit] = hop(near[bit], "dp", dp_size, 1)
    far[z_both] = hop(between, "dp", dp_size, 1)
    late_bits = (z_far | x_bit, z_both | x_bit)
    early_bits = tuple(bit for bit in near if bit not in late_bits)
    early_chips = [bit >> 1 for bit in early_bits]
    late_chips = [bit >> 1 for bit in late_bits]
    early = pl.pallas_call(
        functools.partial(early_kernel, early_chips),
        out_shape=jax.ShapeDtypeStruct((token_count, width), jnp.float32),
        in_specs=vmem(1 + 2 * len(early_bits)),
        out_specs=vmem(1)[0],
        cost_estimate=pl.CostEstimate(
            flops=4 * 2 * token_count * HEADS * HD * width,
            bytes_accessed=2 * HEADS * HD * width,
            transcendentals=0,
        ),
        compiler_params=pltpu.CompilerParams(vmem_limit_bytes=16 * 2**20),
    )(attended, *[near[bit] for bit in early_bits], *[far[bit] for bit in early_bits])
    gate_up_near = jnp.swapaxes(w_gate_up[0], 1, 2)

    some_rows = jax.ShapeDtypeStruct((CAP, width), jnp.bfloat16)
    all_rows = jax.ShapeDtypeStruct((token_count, width), jnp.bfloat16)
    attn_proj, kept, sent, second, last, expert_sum = pl.pallas_call(
        functools.partial(project_kernel, late_chips),
        out_shape=(all_rows, some_rows, some_rows, some_rows, some_rows, all_rows),
        in_specs=smem(1) + vmem(5 + 2 * len(late_bits)),
        out_specs=tuple(vmem(4) + [pl.BlockSpec(memory_space=pl.ANY)] * 2),
        scratch_shapes=[pltpu.VMEM((token_count, width), jnp.float32)],
        cost_estimate=pl.CostEstimate(
            flops=2 * token_count * HEADS * HD * width,
            bytes_accessed=2 * HEADS * HD * width,
            transcendentals=0,
        ),
        compiler_params=pltpu.CompilerParams(vmem_limit_bytes=16 * 2**20),
    )(
        info,
        attended,
        residual[0],
        norm_gain[None],
        select,
        early,
        *[near[bit] for bit in late_bits],
        *[far[bit] for bit in late_bits],
    )

    units = w_down.shape[1]
    row_count = dp_size * CAP

    def dispatch(bit):
        rest = [b for b in bits if b != bit]

        def run(kept, sent):
            gate_up_far = hop(gate_up_near, "dp", dp_size, 1)
            down_far = hop(w_down[0], "dp", dp_size, 1)
            rows = gather_rows(kept, sent, bit, rest, dp_size)
            return rows, gate_up_far, down_far

        return run

    def give_back(bit):
        rest = [b for b in bits if b != bit]

        def run(made, masks):
            return scatter_rows(made, bit, rest, dp_size, masks)

        return run

    branch = info[BRANCH]

    def one_pass(step, carried):
        kept, sent, last, _ = carried
        rows, gate_up_far, down_far = lax.switch(
            branch, [dispatch(bit) for bit in bits], kept, sent
        )
        made, masks = pl.pallas_call(
            expert_kernel,
            out_shape=(
                jax.ShapeDtypeStruct((row_count, width), jnp.bfloat16),
                jax.ShapeDtypeStruct((PASS_COUNT, 1, width), jnp.float32),
            ),
            in_specs=smem(2) + vmem(1) + [pl.BlockSpec(memory_space=pltpu.HBM)] * 4,
            out_specs=tuple(vmem(2)),
            scratch_shapes=[
                pltpu.VMEM((2, units, width), jnp.bfloat16),
                pltpu.VMEM((units, width), jnp.bfloat16),
                pltpu.VMEM((2 * units, row_count), jnp.float32),
                pltpu.VMEM((row_count, units), jnp.bfloat16),
                pltpu.SemaphoreType.DMA((width // 512 + 1,)),
            ],
            cost_estimate=pl.CostEstimate(
                flops=6 * row_count * units * width,
                bytes_accessed=6 * units * width,
                transcendentals=row_count * units,
            ),
            compiler_params=pltpu.CompilerParams(vmem_limit_bytes=26 * 2**20),
        )(info, step[None], rows, gate_up_near, gate_up_far, w_down[0], down_far)
        own, other = lax.switch(branch, [give_back(bit) for bit in bits], made, masks)
        expert_sum, last, kept, sent = pl.pallas_call(
            combine_kernel,
            out_shape=(all_rows, some_rows, some_rows, some_rows),
            in_specs=smem(2) + vmem(6),
            out_specs=tuple(vmem(4)),
            compiler_params=pltpu.CompilerParams(vmem_limit_bytes=8 * 2**20),
        )(info, step[None], own, other, last, second, select, gate_values)
        return kept, sent, last, expert_sum

    carried = (kept, sent, last, expert_sum)
    expert_sum = lax.fori_loop(0, info[PASSES], one_pass, carried)[3]
    return (attn_proj[None], expert_sum[None])


def solution(mesh):
    placed = (
        P("dp", "ctx", None),
        P("dp", "ctx", None),
        P("dp", "ctx", None),
        P("dp", "ctx", None),
        P("dp", None),
        P(),
        P("dp", None, None, "ctx"),
        P("dp", "ctx", None),
        P("dp", "ctx", None),
        P("dp", "ctx", None),
        P("dp", "ctx", None),
        P(),
    )
    dp_size, ctx_size = mesh.shape["dp"], mesh.shape["ctx"]
    small = ctx_size == 2 and dp_size == 2 * HEADS
    return jax.shard_map(
        body_move_rows if small else body_move_weights,
        mesh=mesh,
        in_specs=placed,
        out_specs=(P("dp", "ctx", None), P("dp", "ctx", None)),
        check_vma=False,
    )
```

profile of v0, /device:TPU:0, one launch (start us, length us, event | category | flops | bytes accessed | tf_op | source)
XLA Modules:
  0.0 113.6 jit_solution(256639777927699383)
XLA Ops:
  0.7 4.1 %collective-permute-start.48 = (bf16[64,2048]{1,0:T(8,128)(2,1)}, bf16[64,2048]{1,0:T(8,128)(2,1)S(1)}, u32[]{:S(2)}, u32[]{:S(2)}) collective-permute-start(bf16[64,2048]{1,0:T(8,128)(2,1)} %refs_0_), channel_id=1, source_target_pairs={{0,16},{2,18},{4,20},{6,22},{8,24},{10,26},{12,28},{14,30},{16,0},... | collective-permute-start | bytes 786440 | tf_op jit(solution)/shard_map/ppermute | solution.py:26
  4.8 1.6 %collective-permute-start.49 = (bf16[64,2048]{1,0:T(8,128)(2,1)}, bf16[64,2048]{1,0:T(8,128)(2,1)S(1)}, u32[]{:S(2)}, u32[]{:S(2)}) collective-permute-start(bf16[64,2048]{1,0:T(8,128)(2,1)} %refs_0_), channel_id=1, source_target_pairs={{0,8},{2,10},{4,12},{6,14},{8,0},{10,2},{12,4},{14,6},{16,24},{18,... | collective-permute-start | bytes 786440 | tf_op jit(solution)/shard_map/ppermute | solution.py:26
  6.3 1.5 %collective-permute-start.50 = (bf16[64,2048]{1,0:T(8,128)(2,1)}, bf16[64,2048]{1,0:T(8,128)(2,1)S(1)}, u32[]{:S(2)}, u32[]{:S(2)}) collective-permute-start(bf16[64,2048]{1,0:T(8,128)(2,1)} %refs_0_), channel_id=1, source_target_pairs={{0,4},{2,6},{4,0},{6,2},{8,12},{10,14},{12,8},{14,10},{16,20},{18,... | collective-permute-start | bytes 786440 | tf_op jit(solution)/shard_map/ppermute | solution.py:26
  7.8 3.4 %collective-permute-start.51 = (bf16[128,1024]{1,0:T(8,128)(2,1)}, bf16[128,1024]{1,0:T(8,128)(2,1)S(1)}, u32[]{:S(2)}, u32[]{:S(2)}) collective-permute-start(bf16[128,1024]{1,0:T(8,128)(2,1)} %bitcast.200), channel_id=1, source_target_pairs={{0,1},{2,3},{4,5},{6,7},{8,9},{10,11},{12,13},{14,15},{16,17},{18,... | collective-permute-start | bytes 786440 | tf_op jit(solution)/shard_map/ppermute | solution.py:495
  11.3 1.3 %collective-permute-start.52 = (bf16[128,1024]{1,0:T(8,128)(2,1)}, bf16[128,1024]{1,0:T(8,128)(2,1)S(1)}, u32[]{:S(2)}, u32[]{:S(2)}) collective-permute-start(bf16[128,1024]{1,0:T(8,128)(2,1)} %bitcast.201), channel_id=1, source_target_pairs={{0,1},{2,3},{4,5},{6,7},{8,9},{10,11},{12,13},{14,15},{16,17},{18,... | collective-permute-start | bytes 786440 | tf_op jit(solution)/shard_map/ppermute | solution.py:496
  12.6 0.7 copy.39
  13.3 0.7 copy.40
  14.0 1.2 %pad_maximum_fusion.9.own_vecs = bf16[3,128,1024]{2,1,0:T(8,128)(2,1)S(1)} fusion(bf16[1,128,1024]{2,1,0:T(8,128)(2,1)} %param.22, bf16[1,128,1024]{2,1,0:T(8,128)(2,1)} %param.21, bf16[1,128,1024]{2,1,0:T(8,128)(2,1)} %param.20), kind=kLoop, calls=%fused_computation.123 | loop fusion | flops 786432 | bytes 1572864 | tf_op jit(solution)/shard_map/stack | solution.py:497
  15.2 0.1 pad_add_fusion.numbers
  15.2 1.8 %collective-permute-done.48.refs_1_ = bf16[64,2048]{1,0:T(8,128)(2,1)S(1)} collective-permute-done((bf16[64,2048]{1,0:T(8,128)(2,1)}, bf16[64,2048]{1,0:T(8,128)(2,1)S(1)}, u32[]{:S(2)}, u32[]{:S(2)}) %collective-permute-start.48) | collective-permute-done | bytes 262176 | tf_op jit(solution)/shard_map/ppermute | solution.py:26
  17.0 0.2 collective-permute-done.49.refs_2_
  17.2 1.1 collective-permute-done.51.key_before
  18.3 0.4 collective-permute-start.53
  18.8 1.4 %collective-permute-start.55 = (bf16[64,2048]{1,0:T(8,128)(2,1)S(1)}, bf16[64,2048]{1,0:T(8,128)(2,1)S(1)}, u32[]{:S(2)}, u32[]{:S(2)}) collective-permute-start(bf16[64,2048]{1,0:T(8,128)(2,1)S(1)} %collective-permute-done.48.refs_1_), channel_id=1, source_target_pairs={{0,4},{2,6},{4,0},{6,2},{8,12},{10,14},{12,8},{14,10},{16,20},{18,... | collective-permute-start | bytes 786440 | tf_op jit(solution)/shard_map/ppermute | solution.py:26
  20.2 0.6 collective-permute-start.54
  20.8 1.1 collective-permute-done.52.value_before
  21.9 2.8 %collective-permute-done.53.refs_5_ = bf16[64,2048]{1,0:T(8,128)(2,1)S(1)} collective-permute-done((bf16[64,2048]{1,0:T(8,128)(2,1)S(1)}, bf16[64,2048]{1,0:T(8,128)(2,1)S(1)}, u32[]{:S(2)}, u32[]{:S(2)}) %collective-permute-start.53) | collective-permute-done | bytes 262176 | tf_op jit(solution)/shard_map/ppermute | solution.py:26
  24.7 3.3 %collective-permute-done.55.refs_0_ = bf16[64,2048]{1,0:T(8,128)(2,1)S(1)} collective-permute-done((bf16[64,2048]{1,0:T(8,128)(2,1)S(1)}, bf16[64,2048]{1,0:T(8,128)(2,1)S(1)}, u32[]{:S(2)}, u32[]{:S(2)}) %collective-permute-start.55) | collective-permute-done | bytes 262176 | tf_op jit(solution)/shard_map/ppermute | solution.py:26
  28.0 1.4 %collective-permute-start.62 = (bf16[64,2048]{1,0:T(8,128)(2,1)S(1)}, bf16[64,2048]{1,0:T(8,128)(2,1)S(1)}, u32[]{:S(2)}, u32[]{:S(2)}) collective-permute-start(bf16[64,2048]{1,0:T(8,128)(2,1)S(1)} %collective-permute-done.53.refs_5_), channel_id=1, source_target_pairs={{0,4},{2,6},{4,0},{6,2},{8,12},{10,14},{12,8},{14,10},{16,20},{18,... | collective-permute-start | bytes 786440 | tf_op jit(solution)/shard_map/ppermute | solution.py:26
  29.4 3.7 %shard_map.131 = (bf16[8,128,128]{2,1,0:T(8,128)(2,1)S(1)}, bf16[2,24,128]{2,1,0:T(8,128)(2,1)S(1)}, f32[128,2]{1,0:T(8,128)S(1)}, s32[20]{0:T(128)S(1)}) custom-call(s32[4]{0:T(128)S(1)} %pad_add_fusion.numbers, bf16[3,128,1024]{2,1,0:T(8,128)(2,1)S(1)} %pad_maximum_fusion.9.own_vecs, bf16[128,1024]{1,0:T(8,128)(2,1)S(1)} %collective-permute-done.51.key_before, ...), custom_call_target="tpu_custom_call" | custom-call | flops 2147483648 | bytes 1572864 | tf_op jit(solution)/shard_map/pallas_call | solution.py:526
  33.1 0.5 collective-permute-done.54.refs_4_
  33.6 0.5 collective-permute-start.60
  34.1 0.1 collective-permute-start.61
  34.2 0.4 collective-permute-start.63
  34.7 2.3 %collective-permute-done.62.refs_1_ = bf16[64,2048]{1,0:T(8,128)(2,1)S(1)} collective-permute-done((bf16[64,2048]{1,0:T(8,128)(2,1)S(1)}, bf16[64,2048]{1,0:T(8,128)(2,1)S(1)}, u32[]{:S(2)}, u32[]{:S(2)}) %collective-permute-start.62) | collective-permute-done | bytes 262176 | tf_op jit(solution)/shard_map/ppermute | solution.py:26
  37.0 0.6 fusion.27
  38.3 1.7 %shard_map.132.early = f32[128,2048]{1,0:T(8,128)S(1)} custom-call(bf16[8,128,128]{2,1,0:T(8,128)(2,1)S(1)} %get-tuple-element.262.attended, bf16[64,2048]{1,0:T(8,128)(2,1)S(1)} %copy-done.2, bf16[64,2048]{1,0:T(8,128)(2,1)S(1)} %collective-permute-done.48.refs_1_, bf16[64,2048]{1,0:T(8,128)(2,1)S(1)} %collective-permute-done.49.refs_2_, ...), custom_call_target="tpu_custom_call" | custom-call | flops 2147483648 | bytes 4194304 | tf_op jit(solution)/shard_map/pallas_call | solution.py:560
  40.0 1.7 %shard_map.133 = (bf16[128,2048]{1,0:T(8,128)(2,1)}, bf16[24,2048]{1,0:T(8,128)(2,1)S(1)}, bf16[24,2048]{1,0:T(8,128)(2,1)S(1)}, bf16[24,2048]{1,0:T(8,128)(2,1)...) custom-call(s32[20]{0:T(128)S(1)} %get-tuple-element.477.info, ...), custom_call_target="tpu_custom_call" | custom-call | flops 536870912 | bytes 4194304 | tf_op jit(solution)/shard_map/pallas_call | solution.py:576
  41.8 71.7 %while.18 = (s32[]{:T(128)}, bf16[24,2048]{1,0:T(8,128)(2,1)S(1)}, bf16[24,2048]{1,0:T(8,128)(2,1)S(1)}, bf16[24,2048]{1,0:T(8,128)(2,1)S(1)}, bf16[128,2048]{1,...) while((s32[]{:T(128)}, bf16[24,2048]{1,0:T(8,128)(2,1)S(1)}, ...), condition=%wide.region_7.8_spmd, body=%wide.region_0.7_spmd.sunk | while | flops 3330938880 | bytes 73175896 | solution.py:661
  42.6 33.8 %conditional.4 = (bf16[384,2048]{1,0:T(8,128)(2,1)S(1)}, bf16[2,704,2048]{2,1,0:T(8,128)(2,1)}, bf16[704,2048]{1,0:T(8,128)(2,1)}) conditional(s32[]{:T(128)} %get-tuple-element.504, (bf16[24,2048]{1,0:T(8,128)(2,1)S(1)}, bf16[24,2048]{1,0:T(8,128)(2,1)S(1)}, bf16[2,704,2048]{2,1,0:T(8,128)(2,1)}, ...), branch_computations={%region_1.0_spmd, %region_2.0_spmd, %region_3.0_spmd} | conditional | flops 6684672 | bytes 51118464 | solution.py:625
  42.6 0.6 collective-permute-start.25
  43.2 0.1 collective-permute-start.26
  43.3 1.5 %collective-permute-start.19 = (bf16[24,2048]{1,0:T(8,128)(2,1)S(1)}, bf16[24,2048]{1,0:T(8,128)(2,1)S(1)}, u32[]{:S(2)}, u32[]{:S(2)}) collective-permute-start(bf16[24,2048]{1,0:T(8,128)(2,1)S(1)} %get-tuple-element.177), channel_id=1, source_target_pairs={{0,4},{2,6},{4,0},{6,2},{8,12},{10,14},{12,8},{14,10},{16,20},{18,... | collective-permute-start | bytes 294920 | tf_op jit(solution)/shard_map/while/body/cond/branch_2_fun/ppermute | solution.py:26
  44.8 3.2 %collective-permute-start.20 = (bf16[24,2048]{1,0:T(8,128)(2,1)S(1)}, bf16[24,2048]{1,0:T(8,128)(2,1)S(1)}, u32[]{:S(2)}, u32[]{:S(2)}) collective-permute-start(bf16[24,2048]{1,0:T(8,128)(2,1)S(1)} %get-tuple-element.177), channel_id=1, source_target_pairs={{0,20},{2,22},{4,16},{6,18},{8,28},{10,30},{12,24},{14,26},{16,4},... | collective-permute-start | bytes 294920 | tf_op jit(solution)/shard_map/while/body/cond/branch_2_fun/ppermute | solution.py:26
  48.1 9.2 %collective-permute-done.18 = bf16[24,2048]{1,0:T(8,128)(2,1)S(1)} collective-permute-done((bf16[24,2048]{1,0:T(8,128)(2,1)S(1)}, bf16[24,2048]{1,0:T(8,128)(2,1)S(1)}, u32[]{:S(2)}, u32[]{:S(2)}) %collective-permute-start.18) | collective-permute-done | bytes 98336 | tf_op jit(solution)/shard_map/while/body/cond/branch_2_fun/ppermute | solution.py:26
  57.4 0.1 slice_bitcast_fusion.5
  57.4 0.1 collective-permute-start.21
  57.5 1.6 %collective-permute-start.23 = (bf16[96,1024]{1,0:T(8,128)(2,1)S(1)}, bf16[96,1024]{1,0:T(8,128)(2,1)S(1)}, u32[]{:S(2)}, u32[]{:S(2)}) collective-permute-start(bf16[96,1024]{1,0:T(8,128)(2,1)S(1)} %get-tuple-element.335), channel_id=1, source_target_pairs={{0,1},{1,0},{2,3},{3,2},{4,5},{5,4},{6,7},{7,6},{8,9},{9,8},{10,11... | collective-permute-start | bytes 589832 | tf_op jit(solution)/shard_map/while/body/cond/branch_2_fun/ppermute | solution.py:26
  59.1 5.3 %collective-permute-done.21 = bf16[96,1024]{1,0:T(8,128)(2,1)S(1)} collective-permute-done((bf16[96,1024]{1,0:T(8,128)(2,1)S(1)}, bf16[96,1024]{1,0:T(8,128)(2,1)S(1)}, u32[]{:S(2)}, u32[]{:S(2)}) %collective-permute-start.21) | collective-permute-done | bytes 196640 | tf_op jit(solution)/shard_map/while/body/cond/branch_2_fun/ppermute | solution.py:26
  64.4 0.1 fusion.5
  64.4 1.6 %collective-permute-start.22 = (bf16[2,96,1024]{2,1,0:T(8,128)(2,1)S(1)}, bf16[2,96,1024]{2,1,0:T(8,128)(2,1)S(1)}, u32[]{:S(2)}, u32[]{:S(2)}) collective-permute-start(bf16[2,96,1024]{2,1,0:T(8,128)(2,1)S(1)} %get-tuple-element.332), channel_id=1, source_target_pairs={{0,1},{1,0},{2,3},{3,2},{4,5},{5,4},{6,7},{7,6},{8,9},{9,8},{10,11... | collective-permute-start | bytes 1179656 | tf_op jit(solution)/shard_map/while/body/cond/branch_2_fun/ppermute | solution.py:26
  66.1 0.4 collective-permute-start.24
  66.4 8.3 %collective-permute-done.22 = bf16[2,96,1024]{2,1,0:T(8,128)(2,1)S(1)} collective-permute-done((bf16[2,96,1024]{2,1,0:T(8,128)(2,1)S(1)}, bf16[2,96,1024]{2,1,0:T(8,128)(2,1)S(1)}, u32[]{:S(2)}, u32[]{:S(2)}) %collective-permute-start.22) | collective-permute-done | bytes 393248 | tf_op jit(solution)/shard_map/while/body/cond/branch_2_fun/ppermute | solution.py:26
  74.8 1.4 %collective-permute-done.24 = bf16[2,96,1024]{2,1,0:T(8,128)(2,1)S(1)} collective-permute-done((bf16[2,96,1024]{2,1,0:T(8,128)(2,1)S(1)}, bf16[2,96,1024]{2,1,0:T(8,128)(2,1)S(1)}, u32[]{:S(2)}, u32[]{:S(2)}) %collective-permute-start.24) | collective-permute-done | bytes 393248 | tf_op jit(solution)/shard_map/while/body/cond/branch_2_fun/ppermute | solution.py:26
  76.1 0.1 maximum_maximum_fusion.2
  76.2 0.1 copy.28
  76.4 7.3 %body.6 = (bf16[384,2048]{1,0:T(8,128)(2,1)S(1)}, f32[4,1,2048]{2,1,0:T(1,128)S(1)}) custom-call(s32[20]{0:T(128)S(1)} %get-tuple-element.505.info, s32[1]{0:T(128)} %bitcast.162.step, bf16[384,2048]{1,0:T(8,128)(2,1)S(1)} %get-tuple-element.442.rows, bf16[2,704,2048]{2,1,0:T(8,128)(2,1)} %get-tuple-element.502.gate_up_near, ...), custom_call_target="tpu_custom_call" | custom-call | flops 3321888768 | bytes 8650752 | tf_op jit(solution)/shard_map/while/body/pallas_call | solution.py:628
  83.6 27.3 %conditional.5 = (bf16[24,2048]{1,0:T(8,128)(2,1)S(1)}, bf16[24,2048]{1,0:T(8,128)(2,1)S(1)}) conditional(s32[]{:T(128)} %get-tuple-element.504, (f32[4,1,2048]{2,1,0:T(1,128)S(1)}, bf16[384,2048]{1,0:T(8,128)(2,1)S(1)}) %tuple.96, (f32[4,1,2048]{2,1,0:T(1,128)S(1)}, bf16[384,2048]{1,0:T(8,128)(2,1)S(1)}) %tuple.96, ...), branch_computations={%region_4.4_spmd, %region_5.5_spmd, %region_6.6_spmd} | conditional | flops 2365440 | bytes 13209896 | solution.py:650
  83.7 0.7 collective-permute-start.43
  84.4 1.0 collective-permute-start.41
  85.5 7.3 %collective-permute-done.43 = bf16[2,96,1024]{2,1,0:T(8,128)(2,1)S(1)} collective-permute-done((bf16[2,96,1024]{2,1,0:T(8,128)(2,1)S(1)}, bf16[2,96,1024]{2,1,0:T(8,128)(2,1)S(1)}, u32[]{:S(2)}, u32[]{:S(2)}) %collective-permute-start.43) | collective-permute-done | bytes 393248 | tf_op jit(solution)/shard_map/while/body/cond/branch_2_fun/ppermute | solution.py:26
  92.9 0.6 collective-permute-start.44
  93.5 0.9 collective-permute-done.41
  94.4 0.1 fusion.20
  94.6 1.0 collective-permute-start.42
  95.6 3.0 %collective-permute-done.44 = bf16[96,1024]{1,0:T(8,128)(2,1)S(1)} collective-permute-done((bf16[96,1024]{1,0:T(8,128)(2,1)S(1)}, bf16[96,1024]{1,0:T(8,128)(2,1)S(1)}, u32[]{:S(2)}, u32[]{:S(2)}) %collective-permute-start.44) | collective-permute-done | bytes 196640 | tf_op jit(solution)/shard_map/while/body/cond/branch_2_fun/ppermute | solution.py:26
  98.6 0.1 fusion.22
  98.7 1.6 %collective-permute-done.42 = bf16[96,1024]{1,0:T(8,128)(2,1)S(1)} collective-permute-done((bf16[96,1024]{1,0:T(8,128)(2,1)S(1)}, bf16[96,1024]{1,0:T(8,128)(2,1)S(1)}, u32[]{:S(2)}, u32[]{:S(2)}) %collective-permute-start.42) | collective-permute-done | bytes 196640 | tf_op jit(solution)/shard_map/while/body/cond/branch_2_fun/ppermute | solution.py:26
  100.4 2.4 %collective-permute-start.46 = (bf16[24,2048]{1,0:T(8,128)(2,1)S(1)}, bf16[24,2048]{1,0:T(8,128)(2,1)S(1)}, u32[]{:S(2)}, u32[]{:S(2)}) collective-permute-start(bf16[24,2048]{1,0:T(8,128)(2,1)S(1)} %get-tuple-element.196), channel_id=1, source_target_pairs={{0,4},{2,6},{4,0},{6,2},{8,12},{10,14},{12,8},{14,10},{16,20},{18,... | collective-permute-start | bytes 294920 | tf_op jit(solution)/shard_map/while/body/cond/branch_2_fun/ppermute | solution.py:26
  102.7 0.1 compare_reduce_fusion.8
  102.8 2.5 %collective-permute-start.45 = (bf16[24,2048]{1,0:T(8,128)(2,1)S(1)}, bf16[24,2048]{1,0:T(8,128)(2,1)S(1)}, u32[]{:S(2)}, u32[]{:S(2)}) collective-permute-start(bf16[24,2048]{1,0:T(8,128)(2,1)S(1)} %get-tuple-element.195), channel_id=1, source_target_pairs={{0,16},{2,18},{4,20},{6,22},{8,24},{10,26},{12,28},{14,30},{16,0},... | collective-permute-start | bytes 294920 | tf_op jit(solution)/shard_map/while/body/cond/branch_2_fun/ppermute | solution.py:26
  105.3 3.8 %collective-permute-done.47 = bf16[24,2048]{1,0:T(8,128)(2,1)S(1)} collective-permute-done((bf16[24,2048]{1,0:T(8,128)(2,1)S(1)}, bf16[24,2048]{1,0:T(8,128)(2,1)S(1)}, u32[]{:S(2)}, u32[]{:S(2)}) %collective-permute-start.47) | collective-permute-done | bytes 98336 | tf_op jit(solution)/shard_map/while/body/cond/branch_2_fun/ppermute | solution.py:26
  109.2 1.8 %collective-permute-done.45 = bf16[24,2048]{1,0:T(8,128)(2,1)S(1)} collective-permute-done((bf16[24,2048]{1,0:T(8,128)(2,1)S(1)}, bf16[24,2048]{1,0:T(8,128)(2,1)S(1)}, u32[]{:S(2)}, u32[]{:S(2)}) %collective-permute-start.45) | collective-permute-done | bytes 98336 | tf_op jit(solution)/shard_map/while/body/cond/branch_2_fun/ppermute | solution.py:26
  111.0 1.8 %body.7 = (bf16[128,2048]{1,0:T(8,128)(2,1)}, bf16[24,2048]{1,0:T(8,128)(2,1)S(1)}, bf16[24,2048]{1,0:T(8,128)(2,1)S(1)}, bf16[24,2048]{1,0:T(8,128)(2,1)S(1)}) custom-call(s32[20]{0:T(128)S(1)} %get-tuple-element.505.info, s32[1]{0:T(128)} %bitcast.162.step, bf16[24,2048]{1,0:T(8,128)(2,1)S(1)} %get-tuple-element.447.own, ...), custom_call_target="tpu_custom_call" | custom-call | tf_op jit(solution)/shard_map/while/body/pallas_call | solution.py:651
  (48 shorter events, 0.5 us)
Async XLA Ops:
  0.6 24.1 %copy-start.2 = (bf16[64,2048]{1,0:T(8,128)(2,1)S(1)}, bf16[64,2048]{1,0:T(8,128)(2,1)}, u32[]{:S(2)}) copy-start(bf16[64,2048]{1,0:T(8,128)(2,1)} %refs_0_) | copy-start | bytes 786436
  0.6 14.5 %copy-start.4 = (s32[16]{0:T(128)S(1)}, s32[16]{0:T(128)}, u32[]{:S(2)}) copy-start(s32[16]{0:T(128)} %param.31) | copy-start | bytes 196
  0.7 14.5 %copy-start.3 = (s32[1,1,2]{2,1,0:T(1,128)S(1)}, s32[1,1,2]{2,1,0:T(1,128)}, u32[]{:S(2)}) copy-start(s32[1,1,2]{2,1,0:T(1,128)} %param.30) | copy-start | bytes 28
  0.7 16.3 %collective-permute-start.48 = (bf16[64,2048]{1,0:T(8,128)(2,1)}, bf16[64,2048]{1,0:T(8,128)(2,1)S(1)}, u32[]{:S(2)}, u32[]{:S(2)}) collective-permute-start(bf16[64,2048]{1,0:T(8,128)(2,1)} %refs_0_), channel_id=1, source_target_pairs={{0,16},{2,18},{4,20},{6,22},{8,24},{10,26},{12,28},{14,30},{16,0},... | collective-permute-start | bytes 786440 | tf_op jit(solution)/shard_map/ppermute | solution.py:26
  4.8 12.4 %collective-permute-start.49 = (bf16[64,2048]{1,0:T(8,128)(2,1)}, bf16[64,2048]{1,0:T(8,128)(2,1)S(1)}, u32[]{:S(2)}, u32[]{:S(2)}) collective-permute-start(bf16[64,2048]{1,0:T(8,128)(2,1)} %refs_0_), channel_id=1, source_target_pairs={{0,8},{2,10},{4,12},{6,14},{8,0},{10,2},{12,4},{14,6},{16,24},{18,... | collective-permute-start | bytes 786440 | tf_op jit(solution)/shard_map/ppermute | solution.py:26
  6.3 10.9 %collective-permute-start.50 = (bf16[64,2048]{1,0:T(8,128)(2,1)}, bf16[64,2048]{1,0:T(8,128)(2,1)S(1)}, u32[]{:S(2)}, u32[]{:S(2)}) collective-permute-start(bf16[64,2048]{1,0:T(8,128)(2,1)} %refs_0_), channel_id=1, source_target_pairs={{0,4},{2,6},{4,0},{6,2},{8,12},{10,14},{12,8},{14,10},{16,20},{18,... | collective-permute-start | bytes 786440 | tf_op jit(solution)/shard_map/ppermute | solution.py:26
  7.8 10.5 %collective-permute-start.51 = (bf16[128,1024]{1,0:T(8,128)(2,1)}, bf16[128,1024]{1,0:T(8,128)(2,1)S(1)}, u32[]{:S(2)}, u32[]{:S(2)}) collective-permute-start(bf16[128,1024]{1,0:T(8,128)(2,1)} %bitcast.200), channel_id=1, source_target_pairs={{0,1},{2,3},{4,5},{6,7},{8,9},{10,11},{12,13},{14,15},{16,17},{18,... | collective-permute-start | bytes 786440 | tf_op jit(solution)/shard_map/ppermute | solution.py:495
  11.3 10.6 %collective-permute-start.52 = (bf16[128,1024]{1,0:T(8,128)(2,1)}, bf16[128,1024]{1,0:T(8,128)(2,1)S(1)}, u32[]{:S(2)}, u32[]{:S(2)}) collective-permute-start(bf16[128,1024]{1,0:T(8,128)(2,1)} %bitcast.201), channel_id=1, source_target_pairs={{0,1},{2,3},{4,5},{6,7},{8,9},{10,11},{12,13},{14,15},{16,17},{18,... | collective-permute-start | bytes 786440 | tf_op jit(solution)/shard_map/ppermute | solution.py:496
  18.3 6.4 %collective-permute-start.53 = (bf16[64,2048]{1,0:T(8,128)(2,1)S(1)}, bf16[64,2048]{1,0:T(8,128)(2,1)S(1)}, u32[]{:S(2)}, u32[]{:S(2)}) collective-permute-start(bf16[64,2048]{1,0:T(8,128)(2,1)S(1)} %collective-permute-done.48.refs_1_), channel_id=1, source_target_pairs={{0,8},{2,10},{4,12},{6,14},{8,0},{10,2},{12,4},{14,6},{16,24},{18,... | collective-permute-start | bytes 786440 | tf_op jit(solution)/shard_map/ppermute | solution.py:26
  18.8 9.2 %collective-permute-start.55 = (bf16[64,2048]{1,0:T(8,128)(2,1)S(1)}, bf16[64,2048]{1,0:T(8,128)(2,1)S(1)}, u32[]{:S(2)}, u32[]{:S(2)}) collective-permute-start(bf16[64,2048]{1,0:T(8,128)(2,1)S(1)} %collective-permute-done.48.refs_1_), channel_id=1, source_target_pairs={{0,4},{2,6},{4,0},{6,2},{8,12},{10,14},{12,8},{14,10},{16,20},{18,... | collective-permute-start | bytes 786440 | tf_op jit(solution)/shard_map/ppermute | solution.py:26
  20.2 13.4 %collective-permute-start.54 = (bf16[64,2048]{1,0:T(8,128)(2,1)S(1)}, bf16[64,2048]{1,0:T(8,128)(2,1)S(1)}, u32[]{:S(2)}, u32[]{:S(2)}) collective-permute-start(bf16[64,2048]{1,0:T(8,128)(2,1)S(1)} %collective-permute-done.49.refs_2_), channel_id=1, source_target_pairs={{0,4},{2,6},{4,0},{6,2},{8,12},{10,14},{12,8},{14,10},{16,20},{18,... | collective-permute-start | bytes 786440 | tf_op jit(solution)/shard_map/ppermute | solution.py:26
  20.8 12.8 %collective-permute-start.57 = (bf16[64,2048]{1,0:T(8,128)(2,1)S(1)}, bf16[64,2048]{1,0:T(8,128)(2,1)S(1)}, u32[]{:S(2)}, u32[]{:S(2)}) collective-permute-start(bf16[64,2048]{1,0:T(8,128)(2,1)S(1)} %collective-permute-done.48.refs_1_), channel_id=1, source_target_pairs={{0,2},{2,0},{4,6},{6,4},{8,10},{10,8},{12,14},{14,12},{16,18},{18,... | collective-permute-start | bytes 786440 | tf_op jit(solution)/shard_map/ppermute | solution.py:26
  21.9 12.3 %collective-permute-start.58 = (bf16[64,2048]{1,0:T(8,128)(2,1)S(1)}, bf16[64,2048]{1,0:T(8,128)(2,1)S(1)}, u32[]{:S(2)}, u32[]{:S(2)}) collective-permute-start(bf16[64,2048]{1,0:T(8,128)(2,1)S(1)} %collective-permute-done.49.refs_2_), channel_id=1, source_target_pairs={{0,2},{2,0},{4,6},{6,4},{8,10},{10,8},{12,14},{14,12},{16,18},{18,... | collective-permute-start | bytes 786440 | tf_op jit(solution)/shard_map/ppermute | solution.py:26
  24.7 9.5 %collective-permute-start.56 = (bf16[64,2048]{1,0:T(8,128)(2,1)S(1)}, bf16[64,2048]{1,0:T(8,128)(2,1)S(1)}, u32[]{:S(2)}, u32[]{:S(2)}) collective-permute-start(bf16[64,2048]{1,0:T(8,128)(2,1)S(1)} %copy-done.2), channel_id=1, source_target_pairs={{0,2},{2,0},{4,6},{6,4},{8,10},{10,8},{12,14},{14,12},{16,18},{18,... | collective-permute-start | bytes 786440 | tf_op jit(solution)/shard_map/ppermute | solution.py:26
  28.0 9.0 %collective-permute-start.62 = (bf16[64,2048]{1,0:T(8,128)(2,1)S(1)}, bf16[64,2048]{1,0:T(8,128)(2,1)S(1)}, u32[]{:S(2)}, u32[]{:S(2)}) collective-permute-start(bf16[64,2048]{1,0:T(8,128)(2,1)S(1)} %collective-permute-done.53.refs_5_), channel_id=1, source_target_pairs={{0,4},{2,6},{4,0},{6,2},{8,12},{10,14},{12,8},{14,10},{16,20},{18,... | collective-permute-start | bytes 786440 | tf_op jit(solution)/shard_map/ppermute | solution.py:26
  33.6 4.7 %collective-permute-start.59 = (bf16[64,2048]{1,0:T(8,128)(2,1)S(1)}, bf16[64,2048]{1,0:T(8,128)(2,1)S(1)}, u32[]{:S(2)}, u32[]{:S(2)}) collective-permute-start(bf16[64,2048]{1,0:T(8,128)(2,1)S(1)} %collective-permute-done.50.refs_3_), channel_id=1, source_target_pairs={{0,2},{2,0},{4,6},{6,4},{8,10},{10,8},{12,14},{14,12},{16,18},{18,... | collective-permute-start | bytes 786440 | tf_op jit(solution)/shard_map/ppermute | solution.py:26
  33.6 4.7 %collective-permute-start.60 = (bf16[64,2048]{1,0:T(8,128)(2,1)S(1)}, bf16[64,2048]{1,0:T(8,128)(2,1)}, u32[]{:S(2)}, u32[]{:S(2)}) collective-permute-start(bf16[64,2048]{1,0:T(8,128)(2,1)S(1)} %collective-permute-done.54.refs_4_), channel_id=1, source_target_pairs={{0,2},{2,0},{4,6},{6,4},{8,10},{10,8},{12,14},{14,12},{16,18},{18,... | collective-permute-start | bytes 786440 | tf_op jit(solution)/shard_map/ppermute | solution.py:26
  34.1 4.2 %collective-permute-start.61 = (bf16[64,2048]{1,0:T(8,128)(2,1)S(1)}, bf16[64,2048]{1,0:T(8,128)(2,1)}, u32[]{:S(2)}, u32[]{:S(2)}) collective-permute-start(bf16[64,2048]{1,0:T(8,128)(2,1)S(1)} %collective-permute-done.53.refs_5_), channel_id=1, source_target_pairs={{0,2},{2,0},{4,6},{6,4},{8,10},{10,8},{12,14},{14,12},{16,18},{18,... | collective-permute-start | bytes 786440 | tf_op jit(solution)/shard_map/ppermute | solution.py:26
  34.2 5.8 %collective-permute-start.63 = (bf16[64,2048]{1,0:T(8,128)(2,1)S(1)}, bf16[64,2048]{1,0:T(8,128)(2,1)S(1)}, u32[]{:S(2)}, u32[]{:S(2)}) collective-permute-start(bf16[64,2048]{1,0:T(8,128)(2,1)S(1)} %collective-permute-done.55.refs_0_), channel_id=1, source_target_pairs={{0,2},{2,0},{4,6},{6,4},{8,10},{10,8},{12,14},{14,12},{16,18},{18,... | collective-permute-start | bytes 786440 | tf_op jit(solution)/shard_map/ppermute | solution.py:26
  37.0 3.0 %collective-permute-start.64 = (bf16[64,2048]{1,0:T(8,128)(2,1)S(1)}, bf16[64,2048]{1,0:T(8,128)(2,1)S(1)}, u32[]{:S(2)}, u32[]{:S(2)}) collective-permute-start(bf16[64,2048]{1,0:T(8,128)(2,1)S(1)} %collective-permute-done.62.refs_1_), channel_id=1, source_target_pairs={{0,2},{2,0},{4,6},{6,4},{8,10},{10,8},{12,14},{14,12},{16,18},{18,... | collective-permute-start | bytes 786440 | tf_op jit(solution)/shard_map/ppermute | solution.py:26
  38.3 1.7 %copy-start = (bf16[1,128,2048]{2,1,0:T(8,128)(2,1)S(1)}, bf16[1,128,2048]{2,1,0:T(8,128)(2,1)}, u32[]{:S(2)}) copy-start(bf16[1,128,2048]{2,1,0:T(8,128)(2,1)} %param.23) | copy-start | bytes 1572868
  38.3 1.7 %copy-start.1 = (f32[2048]{0:T(1024)S(1)}, f32[2048]{0:T(1024)}, u32[]{:S(2)}) copy-start(f32[2048]{0:T(1024)} %param.25) | copy-start | bytes 24580
  42.6 33.7 %collective-permute-start.25 = (bf16[2,704,2048]{2,1,0:T(8,128)(2,1)}, bf16[2,704,2048]{2,1,0:T(8,128)(2,1)}, u32[]{:S(2)}, u32[]{:S(2)}) collective-permute-start(bf16[2,704,2048]{2,1,0:T(8,128)(2,1)} %get-tuple-element.178), channel_id=1, source_target_pairs={{0,2},{2,0},{4,6},{6,4},{8,10},{10,8},{12,14},{14,12},{16,18},{18,... | collective-permute-start | bytes 17301512 | tf_op jit(solution)/shard_map/while/body/cond/branch_2_fun/ppermute | solution.py:26
  43.2 33.1 %collective-permute-start.26 = (bf16[704,2048]{1,0:T(8,128)(2,1)}, bf16[704,2048]{1,0:T(8,128)(2,1)}, u32[]{:S(2)}, u32[]{:S(2)}) collective-permute-start(bf16[704,2048]{1,0:T(8,128)(2,1)} %bitcast.187), channel_id=1, source_target_pairs={{0,2},{2,0},{4,6},{6,4},{8,10},{10,8},{12,14},{14,12},{16,18},{18,... | collective-permute-start | bytes 8650760 | tf_op jit(solution)/shard_map/while/body/cond/branch_2_fun/ppermute | solution.py:26
  43.3 14.0 %collective-permute-start.19 = (bf16[24,2048]{1,0:T(8,128)(2,1)S(1)}, bf16[24,2048]{1,0:T(8,128)(2,1)S(1)}, u32[]{:S(2)}, u32[]{:S(2)}) collective-permute-start(bf16[24,2048]{1,0:T(8,128)(2,1)S(1)} %get-tuple-element.177), channel_id=1, source_target_pairs={{0,4},{2,6},{4,0},{6,2},{8,12},{10,14},{12,8},{14,10},{16,20},{18,... | collective-permute-start | bytes 294920 | tf_op jit(solution)/shard_map/while/body/cond/branch_2_fun/ppermute | solution.py:26
  44.8 12.5 %collective-permute-start.20 = (bf16[24,2048]{1,0:T(8,128)(2,1)S(1)}, bf16[24,2048]{1,0:T(8,128)(2,1)S(1)}, u32[]{:S(2)}, u32[]{:S(2)}) collective-permute-start(bf16[24,2048]{1,0:T(8,128)(2,1)S(1)} %get-tuple-element.177), channel_id=1, source_target_pairs={{0,20},{2,22},{4,16},{6,18},{8,28},{10,30},{12,24},{14,26},{16,4},... | collective-permute-start | bytes 294920 | tf_op jit(solution)/shard_map/while/body/cond/branch_2_fun/ppermute | solution.py:26
  48.0 9.3 %collective-permute-start.18 = (bf16[24,2048]{1,0:T(8,128)(2,1)S(1)}, bf16[24,2048]{1,0:T(8,128)(2,1)S(1)}, u32[]{:S(2)}, u32[]{:S(2)}) collective-permute-start(bf16[24,2048]{1,0:T(8,128)(2,1)S(1)} %get-tuple-element.176), channel_id=1, source_target_pairs={{0,16},{2,18},{4,20},{6,22},{8,24},{10,26},{12,28},{14,30},{16,0},... | collective-permute-start | bytes 294920 | tf_op jit(solution)/shard_map/while/body/cond/branch_2_fun/ppermute | solution.py:26
  57.4 6.9 %collective-permute-start.21 = (bf16[96,1024]{1,0:T(8,128)(2,1)S(1)}, bf16[96,1024]{1,0:T(8,128)(2,1)S(1)}, u32[]{:S(2)}, u32[]{:S(2)}) collective-permute-start(bf16[96,1024]{1,0:T(8,128)(2,1)S(1)} %get-tuple-element.336), channel_id=1, source_target_pairs={{0,8},{2,10},{4,12},{6,14},{8,0},{10,2},{12,4},{14,6},{16,24},{18,... | collective-permute-start | bytes 589832 | tf_op jit(solution)/shard_map/while/body/cond/branch_2_fun/ppermute | solution.py:26
  57.5 8.5 %collective-permute-start.23 = (bf16[96,1024]{1,0:T(8,128)(2,1)S(1)}, bf16[96,1024]{1,0:T(8,128)(2,1)S(1)}, u32[]{:S(2)}, u32[]{:S(2)}) collective-permute-start(bf16[96,1024]{1,0:T(8,128)(2,1)S(1)} %get-tuple-element.335), channel_id=1, source_target_pairs={{0,1},{1,0},{2,3},{3,2},{4,5},{5,4},{6,7},{7,6},{8,9},{9,8},{10,11... | collective-permute-start | bytes 589832 | tf_op jit(solution)/shard_map/while/body/cond/branch_2_fun/ppermute | solution.py:26
  64.4 10.3 %collective-permute-start.22 = (bf16[2,96,1024]{2,1,0:T(8,128)(2,1)S(1)}, bf16[2,96,1024]{2,1,0:T(8,128)(2,1)S(1)}, u32[]{:S(2)}, u32[]{:S(2)}) collective-permute-start(bf16[2,96,1024]{2,1,0:T(8,128)(2,1)S(1)} %get-tuple-element.332), channel_id=1, source_target_pairs={{0,1},{1,0},{2,3},{3,2},{4,5},{5,4},{6,7},{7,6},{8,9},{9,8},{10,11... | collective-permute-start | bytes 1179656 | tf_op jit(solution)/shard_map/while/body/cond/branch_2_fun/ppermute | solution.py:26
  66.1 10.0 %collective-permute-start.24 = (bf16[2,96,1024]{2,1,0:T(8,128)(2,1)S(1)}, bf16[2,96,1024]{2,1,0:T(8,128)(2,1)S(1)}, u32[]{:S(2)}, u32[]{:S(2)}) collective-permute-start(bf16[2,96,1024]{2,1,0:T(8,128)(2,1)S(1)} %get-tuple-element.338), channel_id=1, source_target_pairs={{0,8},{2,10},{4,12},{6,14},{8,0},{10,2},{12,4},{14,6},{16,24},{18,... | collective-permute-start | bytes 1179656 | tf_op jit(solution)/shard_map/while/body/cond/branch_2_fun/ppermute | solution.py:26
  83.7 9.1 %collective-permute-start.43 = (bf16[2,96,1024]{2,1,0:T(8,128)(2,1)S(1)}, bf16[2,96,1024]{2,1,0:T(8,128)(2,1)S(1)}, u32[]{:S(2)}, u32[]{:S(2)}) collective-permute-start(bf16[2,96,1024]{2,1,0:T(8,128)(2,1)S(1)} %slice_bitcast_fusion.22), channel_id=1, source_target_pairs={{0,8},{2,10},{4,12},{6,14},{8,0},{10,2},{12,4},{14,6},{16,24},{18,... | collective-permute-start | bytes 1179656 | tf_op jit(solution)/shard_map/while/body/cond/branch_2_fun/ppermute | solution.py:26
  84.4 10.0 %collective-permute-start.41 = (bf16[2,96,1024]{2,1,0:T(8,128)(2,1)S(1)}, bf16[2,96,1024]{2,1,0:T(8,128)(2,1)S(1)}, u32[]{:S(2)}, u32[]{:S(2)}) collective-permute-start(bf16[2,96,1024]{2,1,0:T(8,128)(2,1)S(1)} %slice_bitcast_fusion.24), channel_id=1, source_target_pairs={{0,1},{1,0},{2,3},{3,2},{4,5},{5,4},{6,7},{7,6},{8,9},{9,8},{10,11... | collective-permute-start | bytes 1179656 | tf_op jit(solution)/shard_map/while/body/cond/branch_2_fun/ppermute | solution.py:26
  92.9 5.7 %collective-permute-start.44 = (bf16[96,1024]{1,0:T(8,128)(2,1)S(1)}, bf16[96,1024]{1,0:T(8,128)(2,1)S(1)}, u32[]{:S(2)}, u32[]{:S(2)}) collective-permute-start(bf16[96,1024]{1,0:T(8,128)(2,1)S(1)} %slice_bitcast_fusion.26), channel_id=1, source_target_pairs={{0,1},{1,0},{2,3},{3,2},{4,5},{5,4},{6,7},{7,6},{8,9},{9,8},{10,11... | collective-permute-start | bytes 589832 | tf_op jit(solution)/shard_map/while/body/cond/branch_2_fun/ppermute | solution.py:26
  94.6 5.7 %collective-permute-start.42 = (bf16[96,1024]{1,0:T(8,128)(2,1)S(1)}, bf16[96,1024]{1,0:T(8,128)(2,1)S(1)}, u32[]{:S(2)}, u32[]{:S(2)}) collective-permute-start(bf16[96,1024]{1,0:T(8,128)(2,1)S(1)} %slice_bitcast_fusion.28), channel_id=1, source_target_pairs={{0,8},{2,10},{4,12},{6,14},{8,0},{10,2},{12,4},{14,6},{16,24},{18,... | collective-permute-start | bytes 589832 | tf_op jit(solution)/shard_map/while/body/cond/branch_2_fun/ppermute | solution.py:26
  100.4 5.0 %collective-permute-start.46 = (bf16[24,2048]{1,0:T(8,128)(2,1)S(1)}, bf16[24,2048]{1,0:T(8,128)(2,1)S(1)}, u32[]{:S(2)}, u32[]{:S(2)}) collective-permute-start(bf16[24,2048]{1,0:T(8,128)(2,1)S(1)} %get-tuple-element.196), channel_id=1, source_target_pairs={{0,4},{2,6},{4,0},{6,2},{8,12},{10,14},{12,8},{14,10},{16,20},{18,... | collective-permute-start | bytes 294920 | tf_op jit(solution)/shard_map/while/body/cond/branch_2_fun/ppermute | solution.py:26
  102.7 6.4 %collective-permute-start.47 = (bf16[24,2048]{1,0:T(8,128)(2,1)S(1)}, bf16[24,2048]{1,0:T(8,128)(2,1)S(1)}, u32[]{:S(2)}, u32[]{:S(2)}) collective-permute-start(bf16[24,2048]{1,0:T(8,128)(2,1)S(1)} %get-tuple-element.197), channel_id=1, source_target_pairs={{0,20},{2,22},{4,16},{6,18},{8,28},{10,30},{12,24},{14,26},{16,4},... | collective-permute-start | bytes 294920 | tf_op jit(solution)/shard_map/while/body/cond/branch_2_fun/ppermute | solution.py:26
  102.8 8.1 %collective-permute-start.45 = (bf16[24,2048]{1,0:T(8,128)(2,1)S(1)}, bf16[24,2048]{1,0:T(8,128)(2,1)S(1)}, u32[]{:S(2)}, u32[]{:S(2)}) collective-permute-start(bf16[24,2048]{1,0:T(8,128)(2,1)S(1)} %get-tuple-element.195), channel_id=1, source_target_pairs={{0,16},{2,18},{4,20},{6,22},{8,24},{10,26},{12,28},{14,30},{16,0},... | collective-permute-start | bytes 294920 | tf_op jit(solution)/shard_map/while/body/cond/branch_2_fun/ppermute | solution.py:26
where the time goes:
time: 114 us
  waiting for transfers between devices  55.8 us (49%)
  starting transfers between devices  34 us (30%)
  Pallas kernels  16.2 us (14%)
  local copies, waits for them, and re-layouts  2.32 us (2%)
  other arithmetic  1.91 us (2%)
  loops' own time  1.73 us (2%)
  between operations  1.6 us (1%)
    ppermute x31, waiting for transfers between devices, hop(): return lax.ppermute(array, axis, [(i, i ^ bit) for i in range(size)])  53.6 us
    ppermute x31, starting transfers between devices, hop(): return lax.ppermute(array, axis, [(i, i ^ bit) for i in range(size)])  29.3 us
    pallas_call x1, Pallas kernels, one_pass(): pl.pallas_call(expert_kernel, out_shape=(jax.ShapeDtypeStruct((row_count,...  7.26 us
    pallas_call x1, Pallas kernels, body_move_rows(): pl.pallas_call(functools.partial(attend_kernel, bits), out_shape=(jax.Sha...  3.71 us
    ppermute x1, starting transfers between devices, body_move_rows(): key_before = lax.ppermute(key_vecs[0], 'ctx', [(0, 1)])  3.43 us
  transfers between devices with their start and end apart: 33, of which 18 were waited for; matrix products, arithmetic and copies ran while one was open for 4% of the time, Pallas kernels for 5%

commit v1 on v0

--- a/solution.py
+++ b/solution.py
@@ -549,6 +549,7 @@
     ) = lax.optimization_barrier(
         (near[z_near | x_bit], near[z_far | x_bit], near[z_both], attended)
     )
+    near[z_both | x_bit], select = lax.optimization_barrier((near[z_both | x_bit], select))
     far = {}
     for bit in (0, z_far, z_near, x_bit, z_near | x_bit, z_far | x_bit, z_both | x_bit):
         far[bit] = hop(near[bit], "dp", dp_size, 1)

time: 114 us -> 113 us (level)
  waiting for transfers between devices: 55.8 us -> 51.8 us
  starting transfers between devices: 34 us -> 35.5 us
    ppermute x31, waiting for transfers between devices: 53.6 us -> 49.6 us  [hop(): return lax.ppermute(array, axis, [(i, i ^ bit) for i in range(size)])]
    ppermute x31, starting transfers between devices: 29.3 us -> 30.8 us  [hop(): return lax.ppermute(array, axis, [(i, i ^ bit) for i in range(size)])]
  transfers between devices with their start and end apart: 33 -> 33, of which waited for: 18 -> 20; matrix products, arithmetic and copies ran while one was open for 4% -> 4% of each run, Pallas kernels for 5% -> 5%
where the time goes in v1:
time: 113 us; the launch traced here: 112 us
  waiting for transfers between devices  51.8 us (46%)
  starting transfers between devices  35.5 us (31%)
  Pallas kernels  16.2 us (14%)
  other arithmetic  2.58 us (2%)
  local copies, waits for them, and re-layouts  2.29 us (2%)
  loops' own time  1.68 us (1%)
  between operations  1.56 us (1%)
    ppermute x31, waiting for transfers between devices, hop(): return lax.ppermute(array, axis, [(i, i ^ bit) for i in range(size)])  49.6 us
    ppermute x31, starting transfers between devices, hop(): return lax.ppermute(array, axis, [(i, i ^ bit) for i in range(size)])  30.8 us
    pallas_call x1, Pallas kernels, one_pass(): pl.pallas_call(expert_kernel, out_shape=(jax.ShapeDtypeStruct((row_count,...  7.26 us
    pallas_call x1, Pallas kernels, body_move_rows(): pl.pallas_call(functools.partial(attend_kernel, bits), out_shape=(jax.Sha...  3.71 us
    ppermute x1, starting transfers between devices, body_move_rows(): key_before = lax.ppermute(key_vecs[0], 'ctx', [(0, 1)])  3.43 us
  transfers between devices with their start and end apart: 33, of which 20 were waited for; matrix products, arithmetic and copies ran while one was open for 4% of the time, Pallas kernels for 5%

profile of v1, /device:TPU:0, one launch (start us, length us, event | category | flops | bytes accessed | tf_op | source)
XLA Modules:
  0.0 111.6 jit_solution(7831881864416685325)
XLA Ops:
  0.6 4.1 %collective-permute-start.48 = (bf16[64,2048]{1,0:T(8,128)(2,1)}, bf16[64,2048]{1,0:T(8,128)(2,1)S(1)}, u32[]{:S(2)}, u32[]{:S(2)}) collective-permute-start(bf16[64,2048]{1,0:T(8,128)(2,1)} %refs_0_), channel_id=1, source_target_pairs={{0,16},{2,18},{4,20},{6,22},{8,24},{10,26},{12,28},{14,30},{16,0},... | collective-permute-start | bytes 786440 | tf_op jit(solution)/shard_map/ppermute | solution.py:26
  4.7 1.6 %collective-permute-start.49 = (bf16[64,2048]{1,0:T(8,128)(2,1)}, bf16[64,2048]{1,0:T(8,128)(2,1)S(1)}, u32[]{:S(2)}, u32[]{:S(2)}) collective-permute-start(bf16[64,2048]{1,0:T(8,128)(2,1)} %refs_0_), channel_id=1, source_target_pairs={{0,8},{2,10},{4,12},{6,14},{8,0},{10,2},{12,4},{14,6},{16,24},{18,... | collective-permute-start | bytes 786440 | tf_op jit(solution)/shard_map/ppermute | solution.py:26
  6.3 1.5 %collective-permute-start.50 = (bf16[64,2048]{1,0:T(8,128)(2,1)}, bf16[64,2048]{1,0:T(8,128)(2,1)S(1)}, u32[]{:S(2)}, u32[]{:S(2)}) collective-permute-start(bf16[64,2048]{1,0:T(8,128)(2,1)} %refs_0_), channel_id=1, source_target_pairs={{0,4},{2,6},{4,0},{6,2},{8,12},{10,14},{12,8},{14,10},{16,20},{18,... | collective-permute-start | bytes 786440 | tf_op jit(solution)/shard_map/ppermute | solution.py:26
  7.8 3.4 %collective-permute-start.51 = (bf16[128,1024]{1,0:T(8,128)(2,1)}, bf16[128,1024]{1,0:T(8,128)(2,1)S(1)}, u32[]{:S(2)}, u32[]{:S(2)}) collective-permute-start(bf16[128,1024]{1,0:T(8,128)(2,1)} %bitcast.200), channel_id=1, source_target_pairs={{0,1},{2,3},{4,5},{6,7},{8,9},{10,11},{12,13},{14,15},{16,17},{18,... | collective-permute-start | bytes 786440 | tf_op jit(solution)/shard_map/ppermute | solution.py:495
  11.2 1.3 %collective-permute-start.52 = (bf16[128,1024]{1,0:T(8,128)(2,1)}, bf16[128,1024]{1,0:T(8,128)(2,1)S(1)}, u32[]{:S(2)}, u32[]{:S(2)}) collective-permute-start(bf16[128,1024]{1,0:T(8,128)(2,1)} %bitcast.201), channel_id=1, source_target_pairs={{0,1},{2,3},{4,5},{6,7},{8,9},{10,11},{12,13},{14,15},{16,17},{18,... | collective-permute-start | bytes 786440 | tf_op jit(solution)/shard_map/ppermute | solution.py:496
  12.6 0.7 copy.39
  13.2 0.7 copy.40
  13.9 0.7 pad_add_fusion.numbers
  14.7 1.2 %pad_maximum_fusion.9.own_vecs = bf16[3,128,1024]{2,1,0:T(8,128)(2,1)S(1)} fusion(bf16[1,128,1024]{2,1,0:T(8,128)(2,1)} %param.22, bf16[1,128,1024]{2,1,0:T(8,128)(2,1)} %param.21, bf16[1,128,1024]{2,1,0:T(8,128)(2,1)} %param.20), kind=kLoop, calls=%fused_computation.123 | loop fusion | flops 786432 | bytes 1572864 | tf_op jit(solution)/shard_map/stack | solution.py:497
  15.9 1.1 collective-permute-done.48.refs_1_
  17.0 0.2 collective-permute-done.49.refs_2_
  17.2 1.1 %collective-permute-done.51.key_before = bf16[128,1024]{1,0:T(8,128)(2,1)S(1)} collective-permute-done((bf16[128,1024]{1,0:T(8,128)(2,1)}, bf16[128,1024]{1,0:T(8,128)(2,1)S(1)}, u32[]{:S(2)}, u32[]{:S(2)}) %collective-permute-start.51) | collective-permute-done | bytes 262176 | tf_op jit(solution)/shard_map/ppermute | solution.py:495
  18.3 0.4 collective-permute-start.53
  18.7 1.4 %collective-permute-start.55 = (bf16[64,2048]{1,0:T(8,128)(2,1)S(1)}, bf16[64,2048]{1,0:T(8,128)(2,1)S(1)}, u32[]{:S(2)}, u32[]{:S(2)}) collective-permute-start(bf16[64,2048]{1,0:T(8,128)(2,1)S(1)} %collective-permute-done.48.refs_1_), channel_id=1, source_target_pairs={{0,4},{2,6},{4,0},{6,2},{8,12},{10,14},{12,8},{14,10},{16,20},{18,... | collective-permute-start | bytes 786440 | tf_op jit(solution)/shard_map/ppermute | solution.py:26
  20.2 0.6 collective-permute-start.54
  20.8 1.1 collective-permute-done.52.value_before
  21.9 2.8 %collective-permute-done.53.refs_5_ = bf16[64,2048]{1,0:T(8,128)(2,1)S(1)} collective-permute-done((bf16[64,2048]{1,0:T(8,128)(2,1)S(1)}, bf16[64,2048]{1,0:T(8,128)(2,1)S(1)}, u32[]{:S(2)}, u32[]{:S(2)}) %collective-permute-start.53) | collective-permute-done | bytes 262176 | tf_op jit(solution)/shard_map/ppermute | solution.py:26
  24.7 1.1 collective-permute-start.56
  25.8 2.2 %collective-permute-done.55.refs_0_ = bf16[64,2048]{1,0:T(8,128)(2,1)S(1)} collective-permute-done((bf16[64,2048]{1,0:T(8,128)(2,1)S(1)}, bf16[64,2048]{1,0:T(8,128)(2,1)S(1)}, u32[]{:S(2)}, u32[]{:S(2)}) %collective-permute-start.55) | collective-permute-done | bytes 262176 | tf_op jit(solution)/shard_map/ppermute | solution.py:26
  28.0 3.7 %shard_map.131 = (bf16[8,128,128]{2,1,0:T(8,128)(2,1)S(1)}, bf16[2,24,128]{2,1,0:T(8,128)(2,1)S(1)}, f32[128,2]{1,0:T(8,128)S(1)}, s32[20]{0:T(128)S(1)}) custom-call(s32[4]{0:T(128)S(1)} %pad_add_fusion.numbers, bf16[3,128,1024]{2,1,0:T(8,128)(2,1)S(1)} %pad_maximum_fusion.9.own_vecs, bf16[128,1024]{1,0:T(8,128)(2,1)S(1)} %collective-permute-done.51.key_before, ...), custom_call_target="tpu_custom_call" | custom-call | flops 2147483648 | bytes 1572864 | tf_op jit(solution)/shard_map/pallas_call | solution.py:526
  31.7 1.9 %collective-permute-done.54.refs_4_ = bf16[64,2048]{1,0:T(8,128)(2,1)S(1)} collective-permute-done((bf16[64,2048]{1,0:T(8,128)(2,1)S(1)}, bf16[64,2048]{1,0:T(8,128)(2,1)S(1)}, u32[]{:S(2)}, u32[]{:S(2)}) %collective-permute-start.54) | collective-permute-done | bytes 262176 | tf_op jit(solution)/shard_map/ppermute | solution.py:26
  33.6 0.5 collective-permute-start.61
  34.1 2.8 %collective-permute-done.56.refs_1_ = bf16[64,2048]{1,0:T(8,128)(2,1)S(1)} collective-permute-done((bf16[64,2048]{1,0:T(8,128)(2,1)S(1)}, bf16[64,2048]{1,0:T(8,128)(2,1)S(1)}, u32[]{:S(2)}, u32[]{:S(2)}) %collective-permute-start.56) | collective-permute-done | bytes 262176 | tf_op jit(solution)/shard_map/ppermute | solution.py:26
  37.0 0.5 collective-permute-start.63
  37.5 0.1 collective-permute-start.64
  37.6 0.6 fusion.27
  38.9 0.1 collective-permute-done.62.refs_11_
  38.9 1.7 %shard_map.132.early = f32[128,2048]{1,0:T(8,128)S(1)} custom-call(bf16[8,128,128]{2,1,0:T(8,128)(2,1)S(1)} %get-tuple-element.264.attended, bf16[64,2048]{1,0:T(8,128)(2,1)S(1)} %copy-done.2, bf16[64,2048]{1,0:T(8,128)(2,1)S(1)} %collective-permute-done.48.refs_1_, bf16[64,2048]{1,0:T(8,128)(2,1)S(1)} %collective-permute-done.49.refs_2_, ...), custom_call_target="tpu_custom_call" | custom-call | flops 2147483648 | bytes 4194304 | tf_op jit(solution)/shard_map/pallas_call | solution.py:561
  40.6 1.8 %shard_map.133 = (bf16[128,2048]{1,0:T(8,128)(2,1)}, bf16[24,2048]{1,0:T(8,128)(2,1)S(1)}, bf16[24,2048]{1,0:T(8,128)(2,1)S(1)}, bf16[24,2048]{1,0:T(8,128)(2,1)...) custom-call(s32[20]{0:T(128)S(1)} %get-tuple-element.481.info, ...), custom_call_target="tpu_custom_call" | custom-call | flops 536870912 | bytes 4194304 | tf_op jit(solution)/shard_map/pallas_call | solution.py:577
  42.4 69.1 %while.18 = (s32[]{:T(128)}, bf16[24,2048]{1,0:T(8,128)(2,1)S(1)}, bf16[24,2048]{1,0:T(8,128)(2,1)S(1)}, bf16[24,2048]{1,0:T(8,128)(2,1)S(1)}, bf16[128,2048]{1,...) while((s32[]{:T(128)}, bf16[24,2048]{1,0:T(8,128)(2,1)S(1)}, ...), condition=%wide.region_7.8_spmd, body=%wide.region_0.7_spmd.sunk | while | flops 3330938880 | bytes 73175896 | solution.py:662
  43.2 30.6 %conditional.4 = (bf16[384,2048]{1,0:T(8,128)(2,1)S(1)}, bf16[2,704,2048]{2,1,0:T(8,128)(2,1)}, bf16[704,2048]{1,0:T(8,128)(2,1)}) conditional(s32[]{:T(128)} %get-tuple-element.508, (bf16[24,2048]{1,0:T(8,128)(2,1)S(1)}, bf16[24,2048]{1,0:T(8,128)(2,1)S(1)}, bf16[2,704,2048]{2,1,0:T(8,128)(2,1)}, ...), branch_computations={%region_1.0_spmd, %region_2.0_spmd, %region_3.0_spmd} | conditional | flops 6684672 | bytes 51118464 | solution.py:626
  43.2 0.4 collective-permute-start.7
  43.7 0.1 collective-permute-start.8
  43.8 3.3 %collective-permute-start.1 = (bf16[24,2048]{1,0:T(8,128)(2,1)S(1)}, bf16[24,2048]{1,0:T(8,128)(2,1)S(1)}, u32[]{:S(2)}, u32[]{:S(2)}) collective-permute-start(bf16[24,2048]{1,0:T(8,128)(2,1)S(1)} %get-tuple-element.169), channel_id=1, source_target_pairs={{0,16},{2,18},{4,20},{6,22},{8,24},{10,26},{12,28},{14,30},{16,0},... | collective-permute-start | bytes 294920 | tf_op jit(solution)/shard_map/while/body/cond/branch_0_fun/ppermute | solution.py:26
  47.1 0.6 collective-permute-start
  47.7 8.3 %collective-permute-done = bf16[24,2048]{1,0:T(8,128)(2,1)S(1)} collective-permute-done((bf16[24,2048]{1,0:T(8,128)(2,1)S(1)}, bf16[24,2048]{1,0:T(8,128)(2,1)S(1)}, u32[]{:S(2)}, u32[]{:S(2)}) %collective-permute-start) | collective-permute-done | bytes 98336 | tf_op jit(solution)/shard_map/while/body/cond/branch_0_fun/ppermute | solution.py:26
  56.0 0.1 slice_bitcast_fusion.1
  56.1 1.6 %collective-permute-start.3 = (bf16[96,1024]{1,0:T(8,128)(2,1)S(1)}, bf16[96,1024]{1,0:T(8,128)(2,1)S(1)}, u32[]{:S(2)}, u32[]{:S(2)}) collective-permute-start(bf16[96,1024]{1,0:T(8,128)(2,1)S(1)} %get-tuple-element.324), channel_id=1, source_target_pairs={{0,4},{2,6},{4,0},{6,2},{8,12},{10,14},{12,8},{14,10},{16,20},{18,... | collective-permute-start | bytes 589832 | tf_op jit(solution)/shard_map/while/body/cond/branch_0_fun/ppermute | solution.py:26
  57.7 1.5 %collective-permute-start.5 = (bf16[96,1024]{1,0:T(8,128)(2,1)S(1)}, bf16[96,1024]{1,0:T(8,128)(2,1)S(1)}, u32[]{:S(2)}, u32[]{:S(2)}) collective-permute-start(bf16[96,1024]{1,0:T(8,128)(2,1)S(1)} %get-tuple-element.323), channel_id=1, source_target_pairs={{0,1},{1,0},{2,3},{3,2},{4,5},{5,4},{6,7},{7,6},{8,9},{9,8},{10,11... | collective-permute-start | bytes 589832 | tf_op jit(solution)/shard_map/while/body/cond/branch_0_fun/ppermute | solution.py:26
  59.2 3.3 %collective-permute-done.3 = bf16[96,1024]{1,0:T(8,128)(2,1)S(1)} collective-permute-done((bf16[96,1024]{1,0:T(8,128)(2,1)S(1)}, bf16[96,1024]{1,0:T(8,128)(2,1)S(1)}, u32[]{:S(2)}, u32[]{:S(2)}) %collective-permute-start.3) | collective-permute-done | bytes 196640 | tf_op jit(solution)/shard_map/while/body/cond/branch_0_fun/ppermute | solution.py:26
  62.5 1.6 %collective-permute-start.4 = (bf16[2,96,1024]{2,1,0:T(8,128)(2,1)S(1)}, bf16[2,96,1024]{2,1,0:T(8,128)(2,1)S(1)}, u32[]{:S(2)}, u32[]{:S(2)}) collective-permute-start(bf16[2,96,1024]{2,1,0:T(8,128)(2,1)S(1)} %get-tuple-element.320), channel_id=1, source_target_pairs={{0,1},{1,0},{2,3},{3,2},{4,5},{5,4},{6,7},{7,6},{8,9},{9,8},{10,11... | collective-permute-start | bytes 1179656 | tf_op jit(solution)/shard_map/while/body/cond/branch_0_fun/ppermute | solution.py:26
  64.2 1.6 %collective-permute-start.6 = (bf16[2,96,1024]{2,1,0:T(8,128)(2,1)S(1)}, bf16[2,96,1024]{2,1,0:T(8,128)(2,1)S(1)}, u32[]{:S(2)}, u32[]{:S(2)}) collective-permute-start(bf16[2,96,1024]{2,1,0:T(8,128)(2,1)S(1)} %get-tuple-element.326), channel_id=1, source_target_pairs={{0,4},{2,6},{4,0},{6,2},{8,12},{10,14},{12,8},{14,10},{16,20},{18,... | collective-permute-start | bytes 1179656 | tf_op jit(solution)/shard_map/while/body/cond/branch_0_fun/ppermute | solution.py:26
  65.8 6.4 %collective-permute-done.4 = bf16[2,96,1024]{2,1,0:T(8,128)(2,1)S(1)} collective-permute-done((bf16[2,96,1024]{2,1,0:T(8,128)(2,1)S(1)}, bf16[2,96,1024]{2,1,0:T(8,128)(2,1)S(1)}, u32[]{:S(2)}, u32[]{:S(2)}) %collective-permute-start.4) | collective-permute-done | bytes 393248 | tf_op jit(solution)/shard_map/while/body/cond/branch_0_fun/ppermute | solution.py:26
  72.2 1.4 %collective-permute-done.6 = bf16[2,96,1024]{2,1,0:T(8,128)(2,1)S(1)} collective-permute-done((bf16[2,96,1024]{2,1,0:T(8,128)(2,1)S(1)}, bf16[2,96,1024]{2,1,0:T(8,128)(2,1)S(1)}, u32[]{:S(2)}, u32[]{:S(2)}) %collective-permute-start.6) | collective-permute-done | bytes 393248 | tf_op jit(solution)/shard_map/while/body/cond/branch_0_fun/ppermute | solution.py:26
  73.6 0.1 maximum_maximum_fusion
  73.7 0.1 copy.24
  73.9 7.3 %body.6 = (bf16[384,2048]{1,0:T(8,128)(2,1)S(1)}, f32[4,1,2048]{2,1,0:T(1,128)S(1)}) custom-call(s32[20]{0:T(128)S(1)} %get-tuple-element.509.info, s32[1]{0:T(128)} %bitcast.162.step, bf16[384,2048]{1,0:T(8,128)(2,1)S(1)} %get-tuple-element.446.rows, bf16[2,704,2048]{2,1,0:T(8,128)(2,1)} %get-tuple-element.506.gate_up_near, ...), custom_call_target="tpu_custom_call" | custom-call | flops 3321888768 | bytes 8650752 | tf_op jit(solution)/shard_map/while/body/pallas_call | solution.py:629
  81.1 27.9 %conditional.5 = (bf16[24,2048]{1,0:T(8,128)(2,1)S(1)}, bf16[24,2048]{1,0:T(8,128)(2,1)S(1)}) conditional(s32[]{:T(128)} %get-tuple-element.508, (f32[4,1,2048]{2,1,0:T(1,128)S(1)}, bf16[384,2048]{1,0:T(8,128)(2,1)S(1)}) %tuple.98, (f32[4,1,2048]{2,1,0:T(1,128)S(1)}, bf16[384,2048]{1,0:T(8,128)(2,1)S(1)}) %tuple.98, ...), branch_computations={%region_4.4_spmd, %region_5.5_spmd, %region_6.6_spmd} | conditional | flops 2365440 | bytes 13209896 | solution.py:651
  81.2 1.6 %collective-permute-start.29 = (bf16[2,96,1024]{2,1,0:T(8,128)(2,1)S(1)}, bf16[2,96,1024]{2,1,0:T(8,128)(2,1)S(1)}, u32[]{:S(2)}, u32[]{:S(2)}) collective-permute-start(bf16[2,96,1024]{2,1,0:T(8,128)(2,1)S(1)} %slice_bitcast_fusion.6), channel_id=1, source_target_pairs={{0,4},{2,6},{4,0},{6,2},{8,12},{10,14},{12,8},{14,10},{16,20},{18,... | collective-permute-start | bytes 1179656 | tf_op jit(solution)/shard_map/while/body/cond/branch_0_fun/ppermute | solution.py:26
  82.8 0.6 collective-permute-start.27
  83.4 6.2 %collective-permute-done.29 = bf16[2,96,1024]{2,1,0:T(8,128)(2,1)S(1)} collective-permute-done((bf16[2,96,1024]{2,1,0:T(8,128)(2,1)S(1)}, bf16[2,96,1024]{2,1,0:T(8,128)(2,1)S(1)}, u32[]{:S(2)}, u32[]{:S(2)}) %collective-permute-start.29) | collective-permute-done | bytes 393248 | tf_op jit(solution)/shard_map/while/body/cond/branch_0_fun/ppermute | solution.py:26
  89.7 1.1 %collective-permute-start.30 = (bf16[96,1024]{1,0:T(8,128)(2,1)S(1)}, bf16[96,1024]{1,0:T(8,128)(2,1)S(1)}, u32[]{:S(2)}, u32[]{:S(2)}) collective-permute-start(bf16[96,1024]{1,0:T(8,128)(2,1)S(1)} %slice_bitcast_fusion.10), channel_id=1, source_target_pairs={{0,1},{1,0},{2,3},{3,2},{4,5},{5,4},{6,7},{7,6},{8,9},{9,8},{10,11... | collective-permute-start | bytes 589832 | tf_op jit(solution)/shard_map/while/body/cond/branch_0_fun/ppermute | solution.py:26
  90.8 2.1 %collective-permute-done.27 = bf16[2,96,1024]{2,1,0:T(8,128)(2,1)S(1)} collective-permute-done((bf16[2,96,1024]{2,1,0:T(8,128)(2,1)S(1)}, bf16[2,96,1024]{2,1,0:T(8,128)(2,1)S(1)}, u32[]{:S(2)}, u32[]{:S(2)}) %collective-permute-start.27) | collective-permute-done | bytes 393248 | tf_op jit(solution)/shard_map/while/body/cond/branch_0_fun/ppermute | solution.py:26
  93.0 0.1 fusion.6
  93.2 0.1 collective-permute-start.28
  93.2 2.2 %collective-permute-done.30 = bf16[96,1024]{1,0:T(8,128)(2,1)S(1)} collective-permute-done((bf16[96,1024]{1,0:T(8,128)(2,1)S(1)}, bf16[96,1024]{1,0:T(8,128)(2,1)S(1)}, u32[]{:S(2)}, u32[]{:S(2)}) %collective-permute-start.30) | collective-permute-done | bytes 196640 | tf_op jit(solution)/shard_map/while/body/cond/branch_0_fun/ppermute | solution.py:26
  95.5 3.4 %collective-permute-done.28 = bf16[96,1024]{1,0:T(8,128)(2,1)S(1)} collective-permute-done((bf16[96,1024]{1,0:T(8,128)(2,1)S(1)}, bf16[96,1024]{1,0:T(8,128)(2,1)S(1)}, u32[]{:S(2)}, u32[]{:S(2)}) %collective-permute-start.28) | collective-permute-done | bytes 196640 | tf_op jit(solution)/shard_map/while/body/cond/branch_0_fun/ppermute | solution.py:26
  99.0 2.5 %collective-permute-start.32 = (bf16[24,2048]{1,0:T(8,128)(2,1)S(1)}, bf16[24,2048]{1,0:T(8,128)(2,1)S(1)}, u32[]{:S(2)}, u32[]{:S(2)}) collective-permute-start(bf16[24,2048]{1,0:T(8,128)(2,1)S(1)} %get-tuple-element.184), channel_id=1, source_target_pairs={{0,16},{2,18},{4,20},{6,22},{8,24},{10,26},{12,28},{14,30},{16,0},... | collective-permute-start | bytes 294920 | tf_op jit(solution)/shard_map/while/body/cond/branch_0_fun/ppermute | solution.py:26
  101.4 2.3 %collective-permute-start.33 = (bf16[24,2048]{1,0:T(8,128)(2,1)S(1)}, bf16[24,2048]{1,0:T(8,128)(2,1)S(1)}, u32[]{:S(2)}, u32[]{:S(2)}) collective-permute-start(bf16[24,2048]{1,0:T(8,128)(2,1)S(1)} %get-tuple-element.185), channel_id=1, source_target_pairs={{0,24},{2,26},{4,28},{6,30},{8,16},{10,18},{12,20},{14,22},{16,8},... | collective-permute-start | bytes 294920 | tf_op jit(solution)/shard_map/while/body/cond/branch_0_fun/ppermute | solution.py:26
  103.8 0.1 collective-permute-start.31
  103.9 0.6 collective-permute-done.32
  104.5 3.4 %collective-permute-done.33 = bf16[24,2048]{1,0:T(8,128)(2,1)S(1)} collective-permute-done((bf16[24,2048]{1,0:T(8,128)(2,1)S(1)}, bf16[24,2048]{1,0:T(8,128)(2,1)S(1)}, u32[]{:S(2)}, u32[]{:S(2)}) %collective-permute-start.33) | collective-permute-done | bytes 98336 | tf_op jit(solution)/shard_map/while/body/cond/branch_0_fun/ppermute | solution.py:26
  108.0 1.0 collective-permute-done.31
  109.0 1.8 %body.7 = (bf16[128,2048]{1,0:T(8,128)(2,1)}, bf16[24,2048]{1,0:T(8,128)(2,1)S(1)}, bf16[24,2048]{1,0:T(8,128)(2,1)S(1)}, bf16[24,2048]{1,0:T(8,128)(2,1)S(1)}) custom-call(s32[20]{0:T(128)S(1)} %get-tuple-element.509.info, s32[1]{0:T(128)} %bitcast.162.step, bf16[24,2048]{1,0:T(8,128)(2,1)S(1)} %get-tuple-element.451.own, ...), custom_call_target="tpu_custom_call" | custom-call | tf_op jit(solution)/shard_map/while/body/pallas_call | solution.py:652
  (44 shorter events, 0.6 us)
Async XLA Ops:
  0.6 27.4 %copy-start.2 = (bf16[64,2048]{1,0:T(8,128)(2,1)S(1)}, bf16[64,2048]{1,0:T(8,128)(2,1)}, u32[]{:S(2)}) copy-start(bf16[64,2048]{1,0:T(8,128)(2,1)} %refs_0_) | copy-start | bytes 786436
  0.6 16.3 %collective-permute-start.48 = (bf16[64,2048]{1,0:T(8,128)(2,1)}, bf16[64,2048]{1,0:T(8,128)(2,1)S(1)}, u32[]{:S(2)}, u32[]{:S(2)}) collective-permute-start(bf16[64,2048]{1,0:T(8,128)(2,1)} %refs_0_), channel_id=1, source_target_pairs={{0,16},{2,18},{4,20},{6,22},{8,24},{10,26},{12,28},{14,30},{16,0},... | collective-permute-start | bytes 786440 | tf_op jit(solution)/shard_map/ppermute | solution.py:26
  4.7 12.4 %collective-permute-start.49 = (bf16[64,2048]{1,0:T(8,128)(2,1)}, bf16[64,2048]{1,0:T(8,128)(2,1)S(1)}, u32[]{:S(2)}, u32[]{:S(2)}) collective-permute-start(bf16[64,2048]{1,0:T(8,128)(2,1)} %refs_0_), channel_id=1, source_target_pairs={{0,8},{2,10},{4,12},{6,14},{8,0},{10,2},{12,4},{14,6},{16,24},{18,... | collective-permute-start | bytes 786440 | tf_op jit(solution)/shard_map/ppermute | solution.py:26
  6.3 10.9 %collective-permute-start.50 = (bf16[64,2048]{1,0:T(8,128)(2,1)}, bf16[64,2048]{1,0:T(8,128)(2,1)S(1)}, u32[]{:S(2)}, u32[]{:S(2)}) collective-permute-start(bf16[64,2048]{1,0:T(8,128)(2,1)} %refs_0_), channel_id=1, source_target_pairs={{0,4},{2,6},{4,0},{6,2},{8,12},{10,14},{12,8},{14,10},{16,20},{18,... | collective-permute-start | bytes 786440 | tf_op jit(solution)/shard_map/ppermute | solution.py:26
  7.8 10.5 %collective-permute-start.51 = (bf16[128,1024]{1,0:T(8,128)(2,1)}, bf16[128,1024]{1,0:T(8,128)(2,1)S(1)}, u32[]{:S(2)}, u32[]{:S(2)}) collective-permute-start(bf16[128,1024]{1,0:T(8,128)(2,1)} %bitcast.200), channel_id=1, source_target_pairs={{0,1},{2,3},{4,5},{6,7},{8,9},{10,11},{12,13},{14,15},{16,17},{18,... | collective-permute-start | bytes 786440 | tf_op jit(solution)/shard_map/ppermute | solution.py:495
  11.2 10.6 %collective-permute-start.52 = (bf16[128,1024]{1,0:T(8,128)(2,1)}, bf16[128,1024]{1,0:T(8,128)(2,1)S(1)}, u32[]{:S(2)}, u32[]{:S(2)}) collective-permute-start(bf16[128,1024]{1,0:T(8,128)(2,1)} %bitcast.201), channel_id=1, source_target_pairs={{0,1},{2,3},{4,5},{6,7},{8,9},{10,11},{12,13},{14,15},{16,17},{18,... | collective-permute-start | bytes 786440 | tf_op jit(solution)/shard_map/ppermute | solution.py:496
  18.3 6.4 %collective-permute-start.53 = (bf16[64,2048]{1,0:T(8,128)(2,1)S(1)}, bf16[64,2048]{1,0:T(8,128)(2,1)S(1)}, u32[]{:S(2)}, u32[]{:S(2)}) collective-permute-start(bf16[64,2048]{1,0:T(8,128)(2,1)S(1)} %collective-permute-done.48.refs_1_), channel_id=1, source_target_pairs={{0,8},{2,10},{4,12},{6,14},{8,0},{10,2},{12,4},{14,6},{16,24},{18,... | collective-permute-start | bytes 786440 | tf_op jit(solution)/shard_map/ppermute | solution.py:26
  18.7 9.2 %collective-permute-start.55 = (bf16[64,2048]{1,0:T(8,128)(2,1)S(1)}, bf16[64,2048]{1,0:T(8,128)(2,1)S(1)}, u32[]{:S(2)}, u32[]{:S(2)}) collective-permute-start(bf16[64,2048]{1,0:T(8,128)(2,1)S(1)} %collective-permute-done.48.refs_1_), channel_id=1, source_target_pairs={{0,4},{2,6},{4,0},{6,2},{8,12},{10,14},{12,8},{14,10},{16,20},{18,... | collective-permute-start | bytes 786440 | tf_op jit(solution)/shard_map/ppermute | solution.py:26
  20.2 13.4 %collective-permute-start.54 = (bf16[64,2048]{1,0:T(8,128)(2,1)S(1)}, bf16[64,2048]{1,0:T(8,128)(2,1)S(1)}, u32[]{:S(2)}, u32[]{:S(2)}) collective-permute-start(bf16[64,2048]{1,0:T(8,128)(2,1)S(1)} %collective-permute-done.49.refs_2_), channel_id=1, source_target_pairs={{0,4},{2,6},{4,0},{6,2},{8,12},{10,14},{12,8},{14,10},{16,20},{18,... | collective-permute-start | bytes 786440 | tf_op jit(solution)/shard_map/ppermute | solution.py:26
  20.8 12.8 %collective-permute-start.58 = (bf16[64,2048]{1,0:T(8,128)(2,1)S(1)}, bf16[64,2048]{1,0:T(8,128)(2,1)S(1)}, u32[]{:S(2)}, u32[]{:S(2)}) collective-permute-start(bf16[64,2048]{1,0:T(8,128)(2,1)S(1)} %collective-permute-done.48.refs_1_), channel_id=1, source_target_pairs={{0,2},{2,0},{4,6},{6,4},{8,10},{10,8},{12,14},{14,12},{16,18},{18,... | collective-permute-start | bytes 786440 | tf_op jit(solution)/shard_map/ppermute | solution.py:26
  24.7 12.3 %collective-permute-start.56 = (bf16[64,2048]{1,0:T(8,128)(2,1)S(1)}, bf16[64,2048]{1,0:T(8,128)(2,1)S(1)}, u32[]{:S(2)}, u32[]{:S(2)}) collective-permute-start(bf16[64,2048]{1,0:T(8,128)(2,1)S(1)} %collective-permute-done.53.refs_5_), channel_id=1, source_target_pairs={{0,4},{2,6},{4,0},{6,2},{8,12},{10,14},{12,8},{14,10},{16,20},{18,... | collective-permute-start | bytes 786440 | tf_op jit(solution)/shard_map/ppermute | solution.py:26
  25.8 11.2 %collective-permute-start.59 = (bf16[64,2048]{1,0:T(8,128)(2,1)S(1)}, bf16[64,2048]{1,0:T(8,128)(2,1)S(1)}, u32[]{:S(2)}, u32[]{:S(2)}) collective-permute-start(bf16[64,2048]{1,0:T(8,128)(2,1)S(1)} %collective-permute-done.49.refs_2_), channel_id=1, source_target_pairs={{0,2},{2,0},{4,6},{6,4},{8,10},{10,8},{12,14},{14,12},{16,18},{18,... | collective-permute-start | bytes 786440 | tf_op jit(solution)/shard_map/ppermute | solution.py:26
  28.0 9.5 %collective-permute-start.57 = (bf16[64,2048]{1,0:T(8,128)(2,1)S(1)}, bf16[64,2048]{1,0:T(8,128)(2,1)S(1)}, u32[]{:S(2)}, u32[]{:S(2)}) collective-permute-start(bf16[64,2048]{1,0:T(8,128)(2,1)S(1)} %copy-done.2), channel_id=1, source_target_pairs={{0,2},{2,0},{4,6},{6,4},{8,10},{10,8},{12,14},{14,12},{16,18},{18,... | collective-permute-start | bytes 786440 | tf_op jit(solution)/shard_map/ppermute | solution.py:26
  33.6 5.2 %collective-permute-start.60 = (bf16[64,2048]{1,0:T(8,128)(2,1)S(1)}, bf16[64,2048]{1,0:T(8,128)(2,1)S(1)}, u32[]{:S(2)}, u32[]{:S(2)}) collective-permute-start(bf16[64,2048]{1,0:T(8,128)(2,1)S(1)} %collective-permute-done.50.refs_3_), channel_id=1, source_target_pairs={{0,2},{2,0},{4,6},{6,4},{8,10},{10,8},{12,14},{14,12},{16,18},{18,... | collective-permute-start | bytes 786440 | tf_op jit(solution)/shard_map/ppermute | solution.py:26
  33.6 5.2 %collective-permute-start.61 = (bf16[64,2048]{1,0:T(8,128)(2,1)S(1)}, bf16[64,2048]{1,0:T(8,128)(2,1)}, u32[]{:S(2)}, u32[]{:S(2)}) collective-permute-start(bf16[64,2048]{1,0:T(8,128)(2,1)S(1)} %collective-permute-done.54.refs_4_), channel_id=1, source_target_pairs={{0,2},{2,0},{4,6},{6,4},{8,10},{10,8},{12,14},{14,12},{16,18},{18,... | collective-permute-start | bytes 786440 | tf_op jit(solution)/shard_map/ppermute | solution.py:26
  37.0 2.0 %collective-permute-start.62 = (bf16[64,2048]{1,0:T(8,128)(2,1)S(1)}, bf16[64,2048]{1,0:T(8,128)(2,1)}, u32[]{:S(2)}, u32[]{:S(2)}) collective-permute-start(bf16[64,2048]{1,0:T(8,128)(2,1)S(1)} %collective-permute-done.53.refs_5_), channel_id=1, source_target_pairs={{0,2},{2,0},{4,6},{6,4},{8,10},{10,8},{12,14},{14,12},{16,18},{18,... | collective-permute-start | bytes 786440 | tf_op jit(solution)/shard_map/ppermute | solution.py:26
  37.0 3.6 %collective-permute-start.63 = (bf16[64,2048]{1,0:T(8,128)(2,1)S(1)}, bf16[64,2048]{1,0:T(8,128)(2,1)S(1)}, u32[]{:S(2)}, u32[]{:S(2)}) collective-permute-start(bf16[64,2048]{1,0:T(8,128)(2,1)S(1)} %collective-permute-done.55.refs_0_), channel_id=1, source_target_pairs={{0,2},{2,0},{4,6},{6,4},{8,10},{10,8},{12,14},{14,12},{16,18},{18,... | collective-permute-start | bytes 786440 | tf_op jit(solution)/shard_map/ppermute | solution.py:26
  37.5 3.1 %collective-permute-start.64 = (bf16[64,2048]{1,0:T(8,128)(2,1)S(1)}, bf16[64,2048]{1,0:T(8,128)(2,1)S(1)}, u32[]{:S(2)}, u32[]{:S(2)}) collective-permute-start(bf16[64,2048]{1,0:T(8,128)(2,1)S(1)} %collective-permute-done.56.refs_1_), channel_id=1, source_target_pairs={{0,2},{2,0},{4,6},{6,4},{8,10},{10,8},{12,14},{14,12},{16,18},{18,... | collective-permute-start | bytes 786440 | tf_op jit(solution)/shard_map/ppermute | solution.py:26
  38.8 1.8 %copy-start = (bf16[1,128,2048]{2,1,0:T(8,128)(2,1)S(1)}, bf16[1,128,2048]{2,1,0:T(8,128)(2,1)}, u32[]{:S(2)}) copy-start(bf16[1,128,2048]{2,1,0:T(8,128)(2,1)} %param.23) | copy-start | bytes 1572868
  38.8 1.8 %copy-start.1 = (f32[2048]{0:T(1024)S(1)}, f32[2048]{0:T(1024)}, u32[]{:S(2)}) copy-start(f32[2048]{0:T(1024)} %param.25) | copy-start | bytes 24580
  43.2 30.6 %collective-permute-start.7 = (bf16[2,704,2048]{2,1,0:T(8,128)(2,1)}, bf16[2,704,2048]{2,1,0:T(8,128)(2,1)}, u32[]{:S(2)}, u32[]{:S(2)}) collective-permute-start(bf16[2,704,2048]{2,1,0:T(8,128)(2,1)} %get-tuple-element.170), channel_id=1, source_target_pairs={{0,2},{2,0},{4,6},{6,4},{8,10},{10,8},{12,14},{14,12},{16,18},{18,... | collective-permute-start | bytes 17301512 | tf_op jit(solution)/shard_map/while/body/cond/branch_0_fun/ppermute | solution.py:26
  43.7 30.2 %collective-permute-start.8 = (bf16[704,2048]{1,0:T(8,128)(2,1)}, bf16[704,2048]{1,0:T(8,128)(2,1)}, u32[]{:S(2)}, u32[]{:S(2)}) collective-permute-start(bf16[704,2048]{1,0:T(8,128)(2,1)} %bitcast.185), channel_id=1, source_target_pairs={{0,2},{2,0},{4,6},{6,4},{8,10},{10,8},{12,14},{14,12},{16,18},{18,... | collective-permute-start | bytes 8650760 | tf_op jit(solution)/shard_map/while/body/cond/branch_0_fun/ppermute | solution.py:26
  43.8 12.2 %collective-permute-start.1 = (bf16[24,2048]{1,0:T(8,128)(2,1)S(1)}, bf16[24,2048]{1,0:T(8,128)(2,1)S(1)}, u32[]{:S(2)}, u32[]{:S(2)}) collective-permute-start(bf16[24,2048]{1,0:T(8,128)(2,1)S(1)} %get-tuple-element.169), channel_id=1, source_target_pairs={{0,16},{2,18},{4,20},{6,22},{8,24},{10,26},{12,28},{14,30},{16,0},... | collective-permute-start | bytes 294920 | tf_op jit(solution)/shard_map/while/body/cond/branch_0_fun/ppermute | solution.py:26
  47.1 8.9 %collective-permute-start.2 = (bf16[24,2048]{1,0:T(8,128)(2,1)S(1)}, bf16[24,2048]{1,0:T(8,128)(2,1)S(1)}, u32[]{:S(2)}, u32[]{:S(2)}) collective-permute-start(bf16[24,2048]{1,0:T(8,128)(2,1)S(1)} %get-tuple-element.169), channel_id=1, source_target_pairs={{0,24},{2,26},{4,28},{6,30},{8,16},{10,18},{12,20},{14,22},{16,8},... | collective-permute-start | bytes 294920 | tf_op jit(solution)/shard_map/while/body/cond/branch_0_fun/ppermute | solution.py:26
  47.1 8.9 %collective-permute-start = (bf16[24,2048]{1,0:T(8,128)(2,1)S(1)}, bf16[24,2048]{1,0:T(8,128)(2,1)S(1)}, u32[]{:S(2)}, u32[]{:S(2)}) collective-permute-start(bf16[24,2048]{1,0:T(8,128)(2,1)S(1)} %get-tuple-element.168), channel_id=1, source_target_pairs={{0,8},{2,10},{4,12},{6,14},{8,0},{10,2},{12,4},{14,6},{16,24},{18,... | collective-permute-start | bytes 294920 | tf_op jit(solution)/shard_map/while/body/cond/branch_0_fun/ppermute | solution.py:26
  56.1 6.4 %collective-permute-start.3 = (bf16[96,1024]{1,0:T(8,128)(2,1)S(1)}, bf16[96,1024]{1,0:T(8,128)(2,1)S(1)}, u32[]{:S(2)}, u32[]{:S(2)}) collective-permute-start(bf16[96,1024]{1,0:T(8,128)(2,1)S(1)} %get-tuple-element.324), channel_id=1, source_target_pairs={{0,4},{2,6},{4,0},{6,2},{8,12},{10,14},{12,8},{14,10},{16,20},{18,... | collective-permute-start | bytes 589832 | tf_op jit(solution)/shard_map/while/body/cond/branch_0_fun/ppermute | solution.py:26
  57.7 6.4 %collective-permute-start.5 = (bf16[96,1024]{1,0:T(8,128)(2,1)S(1)}, bf16[96,1024]{1,0:T(8,128)(2,1)S(1)}, u32[]{:S(2)}, u32[]{:S(2)}) collective-permute-start(bf16[96,1024]{1,0:T(8,128)(2,1)S(1)} %get-tuple-element.323), channel_id=1, source_target_pairs={{0,1},{1,0},{2,3},{3,2},{4,5},{5,4},{6,7},{7,6},{8,9},{9,8},{10,11... | collective-permute-start | bytes 589832 | tf_op jit(solution)/shard_map/while/body/cond/branch_0_fun/ppermute | solution.py:26
  62.5 9.6 %collective-permute-start.4 = (bf16[2,96,1024]{2,1,0:T(8,128)(2,1)S(1)}, bf16[2,96,1024]{2,1,0:T(8,128)(2,1)S(1)}, u32[]{:S(2)}, u32[]{:S(2)}) collective-permute-start(bf16[2,96,1024]{2,1,0:T(8,128)(2,1)S(1)} %get-tuple-element.320), channel_id=1, source_target_pairs={{0,1},{1,0},{2,3},{3,2},{4,5},{5,4},{6,7},{7,6},{8,9},{9,8},{10,11... | collective-permute-start | bytes 1179656 | tf_op jit(solution)/shard_map/while/body/cond/branch_0_fun/ppermute | solution.py:26
  64.2 9.4 %collective-permute-start.6 = (bf16[2,96,1024]{2,1,0:T(8,128)(2,1)S(1)}, bf16[2,96,1024]{2,1,0:T(8,128)(2,1)S(1)}, u32[]{:S(2)}, u32[]{:S(2)}) collective-permute-start(bf16[2,96,1024]{2,1,0:T(8,128)(2,1)S(1)} %get-tuple-element.326), channel_id=1, source_target_pairs={{0,4},{2,6},{4,0},{6,2},{8,12},{10,14},{12,8},{14,10},{16,20},{18,... | collective-permute-start | bytes 1179656 | tf_op jit(solution)/shard_map/while/body/cond/branch_0_fun/ppermute | solution.py:26
  81.2 8.5 %collective-permute-start.29 = (bf16[2,96,1024]{2,1,0:T(8,128)(2,1)S(1)}, bf16[2,96,1024]{2,1,0:T(8,128)(2,1)S(1)}, u32[]{:S(2)}, u32[]{:S(2)}) collective-permute-start(bf16[2,96,1024]{2,1,0:T(8,128)(2,1)S(1)} %slice_bitcast_fusion.6), channel_id=1, source_target_pairs={{0,4},{2,6},{4,0},{6,2},{8,12},{10,14},{12,8},{14,10},{16,20},{18,... | collective-permute-start | bytes 1179656 | tf_op jit(solution)/shard_map/while/body/cond/branch_0_fun/ppermute | solution.py:26
  82.8 10.2 %collective-permute-start.27 = (bf16[2,96,1024]{2,1,0:T(8,128)(2,1)S(1)}, bf16[2,96,1024]{2,1,0:T(8,128)(2,1)S(1)}, u32[]{:S(2)}, u32[]{:S(2)}) collective-permute-start(bf16[2,96,1024]{2,1,0:T(8,128)(2,1)S(1)} %slice_bitcast_fusion.8), channel_id=1, source_target_pairs={{0,1},{1,0},{2,3},{3,2},{4,5},{5,4},{6,7},{7,6},{8,9},{9,8},{10,11... | collective-permute-start | bytes 1179656 | tf_op jit(solution)/shard_map/while/body/cond/branch_0_fun/ppermute | solution.py:26
  89.7 5.7 %collective-permute-start.30 = (bf16[96,1024]{1,0:T(8,128)(2,1)S(1)}, bf16[96,1024]{1,0:T(8,128)(2,1)S(1)}, u32[]{:S(2)}, u32[]{:S(2)}) collective-permute-start(bf16[96,1024]{1,0:T(8,128)(2,1)S(1)} %slice_bitcast_fusion.10), channel_id=1, source_target_pairs={{0,1},{1,0},{2,3},{3,2},{4,5},{5,4},{6,7},{7,6},{8,9},{9,8},{10,11... | collective-permute-start | bytes 589832 | tf_op jit(solution)/shard_map/while/body/cond/branch_0_fun/ppermute | solution.py:26
  93.2 5.7 %collective-permute-start.28 = (bf16[96,1024]{1,0:T(8,128)(2,1)S(1)}, bf16[96,1024]{1,0:T(8,128)(2,1)S(1)}, u32[]{:S(2)}, u32[]{:S(2)}) collective-permute-start(bf16[96,1024]{1,0:T(8,128)(2,1)S(1)} %slice_bitcast_fusion.12), channel_id=1, source_target_pairs={{0,4},{2,6},{4,0},{6,2},{8,12},{10,14},{12,8},{14,10},{16,20},{18,... | collective-permute-start | bytes 589832 | tf_op jit(solution)/shard_map/while/body/cond/branch_0_fun/ppermute | solution.py:26
  99.0 5.6 %collective-permute-start.32 = (bf16[24,2048]{1,0:T(8,128)(2,1)S(1)}, bf16[24,2048]{1,0:T(8,128)(2,1)S(1)}, u32[]{:S(2)}, u32[]{:S(2)}) collective-permute-start(bf16[24,2048]{1,0:T(8,128)(2,1)S(1)} %get-tuple-element.184), channel_id=1, source_target_pairs={{0,16},{2,18},{4,20},{6,22},{8,24},{10,26},{12,28},{14,30},{16,0},... | collective-permute-start | bytes 294920 | tf_op jit(solution)/shard_map/while/body/cond/branch_0_fun/ppermute | solution.py:26
  101.4 6.5 %collective-permute-start.33 = (bf16[24,2048]{1,0:T(8,128)(2,1)S(1)}, bf16[24,2048]{1,0:T(8,128)(2,1)S(1)}, u32[]{:S(2)}, u32[]{:S(2)}) collective-permute-start(bf16[24,2048]{1,0:T(8,128)(2,1)S(1)} %get-tuple-element.185), channel_id=1, source_target_pairs={{0,24},{2,26},{4,28},{6,30},{8,16},{10,18},{12,20},{14,22},{16,8},... | collective-permute-start | bytes 294920 | tf_op jit(solution)/shard_map/while/body/cond/branch_0_fun/ppermute | solution.py:26
  103.8 5.1 %collective-permute-start.31 = (bf16[24,2048]{1,0:T(8,128)(2,1)S(1)}, bf16[24,2048]{1,0:T(8,128)(2,1)S(1)}, u32[]{:S(2)}, u32[]{:S(2)}) collective-permute-start(bf16[24,2048]{1,0:T(8,128)(2,1)S(1)} %get-tuple-element.183), channel_id=1, source_target_pairs={{0,8},{2,10},{4,12},{6,14},{8,0},{10,2},{12,4},{14,6},{16,24},{18,... | collective-permute-start | bytes 294920 | tf_op jit(solution)/shard_map/while/body/cond/branch_0_fun/ppermute | solution.py:26
